TPU v7x, 128 devices: a whole 4x4x4 slice. The times are simulated.
128 devices in a mesh: head: 4 (over y_lo, core), ctx: 32 (over x, y_hi, z).
Axes of the slice: x: 4, y: 4 (y_hi: 2, y_lo: 2; y = y_hi * 2 + y_lo), z: 4, core: 2. Of those that a mesh axis runs over, the one named last changes fastest.
Arguments:
- queries: bfloat16 [16384, 5120], P(('head', 'ctx')), may hold values from -160 to 160
- keys: bfloat16 [16384, 1024], P(('head', 'ctx')), may hold values from -13 to 13
- values: bfloat16 [16384, 1024], P(('head', 'ctx')), may hold values from -6 to 6
- selection: int32 [128, 8], P(('head', 'ctx')), may hold values from 0 to 127, as said below
- seg_lengths: int32 [8], replicated, may hold values from 1 to 8192, 16384 in all
Outputs:
- attended: bfloat16 [16384, 5120], P(('head', 'ctx'))
Inputs may be any that keep to these rules, and one draw needn't show every extreme that they name: `selection`: each row b holds 8 different entries, among them b itself. Its entries lie in 8 different classes of entry % 32. An entry greater than b occurs only where its class holds no block up to b.
All inputs are finite; a program needn't handle non-finite values.
Results may differ from a plain program's by a relative error of at most 0.0039.
Values may be sent and summed in bfloat16 or wider, within the bound.
No kernel may reach another device: no remote copies, remote signals or barrier semaphores. Data moves between devices by JAX's collectives and lax.ppermute only.
A program may use at most 128 MiB of HBM per device.

v0:
```python
import jax
import jax.numpy as jnp
from jax import lax
from jax.sharding import PartitionSpec as P

HQ = 40
HK = 8
DH = 128
BLOCK = 128


neg_fill = -1e30


def passed_along(value, axis, steps):
    count = lax.axis_size(axis)
    pairs = [(source, (source + steps) % count) for source in range(count)]
    return lax.ppermute(value, axis, pairs)


def body(queries, keys, values, selection, seg_lengths):
    ctx_count = lax.axis_size("ctx")
    ctx_index = lax.axis_index("ctx")
    tok_dev = queries.shape[0]
    per_shard = tok_dev // BLOCK
    group = HQ // HK
    scale = DH ** (-0.5)
    local_q, local_k, local_v = (
        lax.all_to_all(queries, "head", split_axis=1, concat_axis=0, tiled=True),
        lax.all_to_all(keys, "head", split_axis=1, concat_axis=0, tiled=True),
        lax.all_to_all(values, "head", split_axis=1, concat_axis=0, tiled=True),
    )
    picks = lax.all_gather(selection, "head", axis=0, tiled=True)
    block_count = picks.shape[0]
    kv_local = local_k.shape[1] // DH
    width = local_k.shape[1]
    kv_pair = jnp.concatenate([local_k, local_v], axis=1)
    query_tiles = local_q.reshape(block_count, BLOCK, kv_local, group, DH)
    ends = jnp.cumsum(seg_lengths)

    def document(positions):
        return jnp.sum((positions[..., None] >= ends).astype(jnp.int32), axis=-1)

    rows_here = jnp.arange(block_count * BLOCK, dtype=jnp.int32)
    query_pos = (
        (rows_here // tok_dev * ctx_count + ctx_index) * tok_dev + rows_here % tok_dev
    ).reshape(block_count, BLOCK)
    query_doc = document(query_pos)
    owner = picks // per_shard % ctx_count
    in_piece = picks // per_shard // ctx_count * per_shard + picks % per_shard
    offsets = jnp.arange(BLOCK, dtype=jnp.int32)

    def attend(state, piece, source):
        top, total, accum = state
        hit = owner == source
        chosen = jnp.sum(jnp.where(hit, picks, 0), axis=1)
        present = jnp.any(hit, axis=1)
        inner = jnp.sum(jnp.where(hit, in_piece, 0), axis=1)
        tiles = piece.reshape(-1, BLOCK, 2 * width)[inner]
        key_tiles = tiles[:, :, :width].reshape(block_count, BLOCK, kv_local, DH)
        value_tiles = tiles[:, :, width:].reshape(block_count, BLOCK, kv_local, DH)
        key_pos = chosen[:, None] * BLOCK + offsets[None, :]
        allowed = (
            present[:, None, None]
            & (key_pos[:, None, :] <= query_pos[:, :, None])
            & (document(key_pos)[:, None, :] == query_doc[:, :, None])
        )
        allowed = allowed[:, :, None, None, :]
        scores = (
            jnp.einsum(
                "bqhgd,bkhd->bqhgk", query_tiles, key_tiles, preferred_element_type=jnp.float32
            )
            * scale
        )
        scores = jnp.where(allowed, scores, neg_fill)
        new_top = jnp.maximum(top, jnp.max(scores, axis=-1))
        shrink = jnp.exp(top - new_top)
        expo = jnp.where(allowed, jnp.exp(scores - new_top[..., None]), 0.0)
        total = total * shrink + jnp.sum(expo, axis=-1)
        accum = accum * shrink[..., None] + jnp.einsum(
            "bqhgk,bkhd->bqhgd",
            expo.astype(jnp.bfloat16),
            value_tiles,
            preferred_element_type=jnp.float32,
        )
        return (new_top, total, accum)

    start_top = jnp.full((block_count, BLOCK, kv_local, group), neg_fill, jnp.float32)
    start_total = jnp.zeros((block_count, BLOCK, kv_local, group), jnp.float32)
    start_accum = jnp.zeros((block_count, BLOCK, kv_local, group, DH), jnp.float32)
    state = attend((start_top, start_total, start_accum), kv_pair, ctx_index)

    def one_hop(step, carry):
        state_now, piece = carry
        piece = passed_along(piece, "ctx", 1)
        state_now = attend(state_now, piece, (ctx_index - step) % ctx_count)
        return (state_now, piece)

    state, piece = lax.fori_loop(1, ctx_count, one_hop, (state, kv_pair))
    top, total, accum = state
    mixed = (
        (accum / total[..., None])
        .astype(jnp.bfloat16)
        .reshape(block_count * BLOCK, local_q.shape[1])
    )
    return lax.all_to_all(mixed, "head", split_axis=0, concat_axis=1, tiled=True)


def solution(mesh):
    return jax.shard_map(
        body,
        mesh=mesh,
        in_specs=(
            P(("head", "ctx"), None),
            P(("head", "ctx"), None),
            P(("head", "ctx"), None),
            P(("head", "ctx"), None),
            P(),
        ),
        out_specs=P(("head", "ctx"), None),
        check_vma=False,
    )
```

profile of v0, /device:TPU:1, one launch (start us, length us, event | category | flops | bytes accessed | tf_op | source)
XLA Modules:
  0.0 905.5 jit_solution(12073559056198729353)
XLA Ops:
  33.8 13.0 %all-to-all-done.2 = bf16[128,4,1280]{0,2,1:T(8,128)(2,1)S(1)} async-done(((bf16[128,4,1280]{0,2,1:T(8,128)(2,1)}), bf16[128,4,1280]{0,2,1:T(8,128)(2,1)S(1)}, u32[]{:S(2)}, u32[]{:S(2)}) %all-to-all-start.2) | async-done | bytes 1310752 | tf_op jit(solution)/shard_map/all_to_all | solution.py:29
  50.5 797.0 %while.23 = (s32[]{:T(128)}, f32[4,128,2,5]{1,3,2,0:T(8,128)S(1)}, f32[4,128,2,5]{1,3,2,0:T(8,128)S(1)}, f32[4,128,2,5,128]{1,4,3,2,0:T(8,128)S(1)}, bf16[512,51...) while((s32[]{:T(128)}, f32[4,128,2,5]{1,3,2,0:T(8,128)S(1)}, ...), condition=%wide.region_15.16_spmd.clone.clone, body=%wide.region_8.15_spmd.clone.clone.sunk | while | flops 345668800 | bytes 21844916 | solution.py:99
  53.6 17.3 %collective-permute-done = bf16[512,512]{1,0:T(8,128)(2,1)S(1)} collective-permute-done((bf16[512,512]{1,0:T(8,128)(2,1)}, bf16[512,512]{1,0:T(8,128)(2,1)S(1)}, u32[]{:S(2)}, u32[]{:S(2)}) %collective-permute-start) | collective-permute-done | bytes 524320 | tf_op jit(solution)/shard_map/while/body/eval_jaxpr/ppermute | solution.py:18
  82.3 16.6 %collective-permute-done = bf16[512,512]{1,0:T(8,128)(2,1)S(1)} collective-permute-done((bf16[512,512]{1,0:T(8,128)(2,1)}, bf16[512,512]{1,0:T(8,128)(2,1)S(1)}, u32[]{:S(2)}, u32[]{:S(2)}) %collective-permute-start) | collective-permute-done | bytes 524320 | tf_op jit(solution)/shard_map/while/body/eval_jaxpr/ppermute | solution.py:18
  110.4 15.7 %collective-permute-done = bf16[512,512]{1,0:T(8,128)(2,1)S(1)} collective-permute-done((bf16[512,512]{1,0:T(8,128)(2,1)}, bf16[512,512]{1,0:T(8,128)(2,1)S(1)}, u32[]{:S(2)}, u32[]{:S(2)}) %collective-permute-start) | collective-permute-done | bytes 524320 | tf_op jit(solution)/shard_map/while/body/eval_jaxpr/ppermute | solution.py:18
  137.5 14.8 %collective-permute-done = bf16[512,512]{1,0:T(8,128)(2,1)S(1)} collective-permute-done((bf16[512,512]{1,0:T(8,128)(2,1)}, bf16[512,512]{1,0:T(8,128)(2,1)S(1)}, u32[]{:S(2)}, u32[]{:S(2)}) %collective-permute-start) | collective-permute-done | bytes 524320 | tf_op jit(solution)/shard_map/while/body/eval_jaxpr/ppermute | solution.py:18
  163.7 13.9 %collective-permute-done = bf16[512,512]{1,0:T(8,128)(2,1)S(1)} collective-permute-done((bf16[512,512]{1,0:T(8,128)(2,1)}, bf16[512,512]{1,0:T(8,128)(2,1)S(1)}, u32[]{:S(2)}, u32[]{:S(2)}) %collective-permute-start) | collective-permute-done | bytes 524320 | tf_op jit(solution)/shard_map/while/body/eval_jaxpr/ppermute | solution.py:18
  189.0 12.7 %collective-permute-done = bf16[512,512]{1,0:T(8,128)(2,1)S(1)} collective-permute-done((bf16[512,512]{1,0:T(8,128)(2,1)}, bf16[512,512]{1,0:T(8,128)(2,1)S(1)}, u32[]{:S(2)}, u32[]{:S(2)}) %collective-permute-start) | collective-permute-done | bytes 524320 | tf_op jit(solution)/shard_map/while/body/eval_jaxpr/ppermute | solution.py:18
  213.2 12.7 %collective-permute-done = bf16[512,512]{1,0:T(8,128)(2,1)S(1)} collective-permute-done((bf16[512,512]{1,0:T(8,128)(2,1)}, bf16[512,512]{1,0:T(8,128)(2,1)S(1)}, u32[]{:S(2)}, u32[]{:S(2)}) %collective-permute-start) | collective-permute-done | bytes 524320 | tf_op jit(solution)/shard_map/while/body/eval_jaxpr/ppermute | solution.py:18
  237.3 12.7 %collective-permute-done = bf16[512,512]{1,0:T(8,128)(2,1)S(1)} collective-permute-done((bf16[512,512]{1,0:T(8,128)(2,1)}, bf16[512,512]{1,0:T(8,128)(2,1)S(1)}, u32[]{:S(2)}, u32[]{:S(2)}) %collective-permute-start) | collective-permute-done | bytes 524320 | tf_op jit(solution)/shard_map/while/body/eval_jaxpr/ppermute | solution.py:18
  261.4 12.7 %collective-permute-done = bf16[512,512]{1,0:T(8,128)(2,1)S(1)} collective-permute-done((bf16[512,512]{1,0:T(8,128)(2,1)}, bf16[512,512]{1,0:T(8,128)(2,1)S(1)}, u32[]{:S(2)}, u32[]{:S(2)}) %collective-permute-start) | collective-permute-done | bytes 524320 | tf_op jit(solution)/shard_map/while/body/eval_jaxpr/ppermute | solution.py:18
  285.5 12.7 %collective-permute-done = bf16[512,512]{1,0:T(8,128)(2,1)S(1)} collective-permute-done((bf16[512,512]{1,0:T(8,128)(2,1)}, bf16[512,512]{1,0:T(8,128)(2,1)S(1)}, u32[]{:S(2)}, u32[]{:S(2)}) %collective-permute-start) | collective-permute-done | bytes 524320 | tf_op jit(solution)/shard_map/while/body/eval_jaxpr/ppermute | solution.py:18
  309.6 12.7 %collective-permute-done = bf16[512,512]{1,0:T(8,128)(2,1)S(1)} collective-permute-done((bf16[512,512]{1,0:T(8,128)(2,1)}, bf16[512,512]{1,0:T(8,128)(2,1)S(1)}, u32[]{:S(2)}, u32[]{:S(2)}) %collective-permute-start) | collective-permute-done | bytes 524320 | tf_op jit(solution)/shard_map/while/body/eval_jaxpr/ppermute | solution.py:18
  333.8 12.7 %collective-permute-done = bf16[512,512]{1,0:T(8,128)(2,1)S(1)} collective-permute-done((bf16[512,512]{1,0:T(8,128)(2,1)}, bf16[512,512]{1,0:T(8,128)(2,1)S(1)}, u32[]{:S(2)}, u32[]{:S(2)}) %collective-permute-start) | collective-permute-done | bytes 524320 | tf_op jit(solution)/shard_map/while/body/eval_jaxpr/ppermute | solution.py:18
  357.9 12.7 %collective-permute-done = bf16[512,512]{1,0:T(8,128)(2,1)S(1)} collective-permute-done((bf16[512,512]{1,0:T(8,128)(2,1)}, bf16[512,512]{1,0:T(8,128)(2,1)S(1)}, u32[]{:S(2)}, u32[]{:S(2)}) %collective-permute-start) | collective-permute-done | bytes 524320 | tf_op jit(solution)/shard_map/while/body/eval_jaxpr/ppermute | solution.py:18
  382.0 12.7 %collective-permute-done = bf16[512,512]{1,0:T(8,128)(2,1)S(1)} collective-permute-done((bf16[512,512]{1,0:T(8,128)(2,1)}, bf16[512,512]{1,0:T(8,128)(2,1)S(1)}, u32[]{:S(2)}, u32[]{:S(2)}) %collective-permute-start) | collective-permute-done | bytes 524320 | tf_op jit(solution)/shard_map/while/body/eval_jaxpr/ppermute | solution.py:18
  406.1 12.7 %collective-permute-done = bf16[512,512]{1,0:T(8,128)(2,1)S(1)} collective-permute-done((bf16[512,512]{1,0:T(8,128)(2,1)}, bf16[512,512]{1,0:T(8,128)(2,1)S(1)}, u32[]{:S(2)}, u32[]{:S(2)}) %collective-permute-start) | collective-permute-done | bytes 524320 | tf_op jit(solution)/shard_map/while/body/eval_jaxpr/ppermute | solution.py:18
  430.2 12.7 %collective-permute-done = bf16[512,512]{1,0:T(8,128)(2,1)S(1)} collective-permute-done((bf16[512,512]{1,0:T(8,128)(2,1)}, bf16[512,512]{1,0:T(8,128)(2,1)S(1)}, u32[]{:S(2)}, u32[]{:S(2)}) %collective-permute-start) | collective-permute-done | bytes 524320 | tf_op jit(solution)/shard_map/while/body/eval_jaxpr/ppermute | solution.py:18
  454.4 12.7 %collective-permute-done = bf16[512,512]{1,0:T(8,128)(2,1)S(1)} collective-permute-done((bf16[512,512]{1,0:T(8,128)(2,1)}, bf16[512,512]{1,0:T(8,128)(2,1)S(1)}, u32[]{:S(2)}, u32[]{:S(2)}) %collective-permute-start) | collective-permute-done | bytes 524320 | tf_op jit(solution)/shard_map/while/body/eval_jaxpr/ppermute | solution.py:18
  478.5 12.7 %collective-permute-done = bf16[512,512]{1,0:T(8,128)(2,1)S(1)} collective-permute-done((bf16[512,512]{1,0:T(8,128)(2,1)}, bf16[512,512]{1,0:T(8,128)(2,1)S(1)}, u32[]{:S(2)}, u32[]{:S(2)}) %collective-permute-start) | collective-permute-done | bytes 524320 | tf_op jit(solution)/shard_map/while/body/eval_jaxpr/ppermute | solution.py:18
  502.6 13.7 %collective-permute-done = bf16[512,512]{1,0:T(8,128)(2,1)S(1)} collective-permute-done((bf16[512,512]{1,0:T(8,128)(2,1)}, bf16[512,512]{1,0:T(8,128)(2,1)S(1)}, u32[]{:S(2)}, u32[]{:S(2)}) %collective-permute-start) | collective-permute-done | bytes 524320 | tf_op jit(solution)/shard_map/while/body/eval_jaxpr/ppermute | solution.py:18
  527.7 14.7 %collective-permute-done = bf16[512,512]{1,0:T(8,128)(2,1)S(1)} collective-permute-done((bf16[512,512]{1,0:T(8,128)(2,1)}, bf16[512,512]{1,0:T(8,128)(2,1)S(1)}, u32[]{:S(2)}, u32[]{:S(2)}) %collective-permute-start) | collective-permute-done | bytes 524320 | tf_op jit(solution)/shard_map/while/body/eval_jaxpr/ppermute | solution.py:18
  553.9 15.8 %collective-permute-done = bf16[512,512]{1,0:T(8,128)(2,1)S(1)} collective-permute-done((bf16[512,512]{1,0:T(8,128)(2,1)}, bf16[512,512]{1,0:T(8,128)(2,1)S(1)}, u32[]{:S(2)}, u32[]{:S(2)}) %collective-permute-start) | collective-permute-done | bytes 524320 | tf_op jit(solution)/shard_map/while/body/eval_jaxpr/ppermute | solution.py:18
  581.1 16.9 %collective-permute-done = bf16[512,512]{1,0:T(8,128)(2,1)S(1)} collective-permute-done((bf16[512,512]{1,0:T(8,128)(2,1)}, bf16[512,512]{1,0:T(8,128)(2,1)S(1)}, u32[]{:S(2)}, u32[]{:S(2)}) %collective-permute-start) | collective-permute-done | bytes 524320 | tf_op jit(solution)/shard_map/while/body/eval_jaxpr/ppermute | solution.py:18
  609.4 18.0 %collective-permute-done = bf16[512,512]{1,0:T(8,128)(2,1)S(1)} collective-permute-done((bf16[512,512]{1,0:T(8,128)(2,1)}, bf16[512,512]{1,0:T(8,128)(2,1)S(1)}, u32[]{:S(2)}, u32[]{:S(2)}) %collective-permute-start) | collective-permute-done | bytes 524320 | tf_op jit(solution)/shard_map/while/body/eval_jaxpr/ppermute | solution.py:18
  638.8 17.8 %collective-permute-done = bf16[512,512]{1,0:T(8,128)(2,1)S(1)} collective-permute-done((bf16[512,512]{1,0:T(8,128)(2,1)}, bf16[512,512]{1,0:T(8,128)(2,1)S(1)}, u32[]{:S(2)}, u32[]{:S(2)}) %collective-permute-start) | collective-permute-done | bytes 524320 | tf_op jit(solution)/shard_map/while/body/eval_jaxpr/ppermute | solution.py:18
  668.1 16.9 %collective-permute-done = bf16[512,512]{1,0:T(8,128)(2,1)S(1)} collective-permute-done((bf16[512,512]{1,0:T(8,128)(2,1)}, bf16[512,512]{1,0:T(8,128)(2,1)S(1)}, u32[]{:S(2)}, u32[]{:S(2)}) %collective-permute-start) | collective-permute-done | bytes 524320 | tf_op jit(solution)/shard_map/while/body/eval_jaxpr/ppermute | solution.py:18
  696.4 16.0 %collective-permute-done = bf16[512,512]{1,0:T(8,128)(2,1)S(1)} collective-permute-done((bf16[512,512]{1,0:T(8,128)(2,1)}, bf16[512,512]{1,0:T(8,128)(2,1)S(1)}, u32[]{:S(2)}, u32[]{:S(2)}) %collective-permute-start) | collective-permute-done | bytes 524320 | tf_op jit(solution)/shard_map/while/body/eval_jaxpr/ppermute | solution.py:18
  723.8 15.1 %collective-permute-done = bf16[512,512]{1,0:T(8,128)(2,1)S(1)} collective-permute-done((bf16[512,512]{1,0:T(8,128)(2,1)}, bf16[512,512]{1,0:T(8,128)(2,1)S(1)}, u32[]{:S(2)}, u32[]{:S(2)}) %collective-permute-start) | collective-permute-done | bytes 524320 | tf_op jit(solution)/shard_map/while/body/eval_jaxpr/ppermute | solution.py:18
  750.3 14.1 %collective-permute-done = bf16[512,512]{1,0:T(8,128)(2,1)S(1)} collective-permute-done((bf16[512,512]{1,0:T(8,128)(2,1)}, bf16[512,512]{1,0:T(8,128)(2,1)S(1)}, u32[]{:S(2)}, u32[]{:S(2)}) %collective-permute-start) | collective-permute-done | bytes 524320 | tf_op jit(solution)/shard_map/while/body/eval_jaxpr/ppermute | solution.py:18
  775.9 13.2 %collective-permute-done = bf16[512,512]{1,0:T(8,128)(2,1)S(1)} collective-permute-done((bf16[512,512]{1,0:T(8,128)(2,1)}, bf16[512,512]{1,0:T(8,128)(2,1)S(1)}, u32[]{:S(2)}, u32[]{:S(2)}) %collective-permute-start) | collective-permute-done | bytes 524320 | tf_op jit(solution)/shard_map/while/body/eval_jaxpr/ppermute | solution.py:18
  850.5 52.7 %all_to_all.73 = bf16[4,128,1280]{2,1,0:T(8,128)(2,1)S(1)} all-to-all(bf16[4,128,1280]{2,1,0:T(8,128)(2,1)S(1)} %copy.88), channel_id=1, replica_groups=mesh['head'=4,'ctx'=32] {'head'}, dimensions={0} | all-to-all | bytes 2621440 | tf_op jit(solution)/shard_map/all_to_all | solution.py:106
  (693 shorter events, 421.3 us)
Async XLA Ops:
  2.1 15.2 %all-to-all-start = ((bf16[128,4,256]{2,0,1:T(8,128)(2,1)}), bf16[128,4,256]{2,0,1:T(8,128)(2,1)S(1)}, u32[]{:S(2)}, u32[]{:S(2)}) async-start(bf16[128,4,256]{2,0,1:T(8,128)(2,1)} %copy.78), calls=%async_computation | async-start | bytes 524288 | tf_op jit(solution)/shard_map/all_to_all | solution.py:30
  26.0 20.8 %all-to-all-start.2 = ((bf16[128,4,1280]{0,2,1:T(8,128)(2,1)}), bf16[128,4,1280]{0,2,1:T(8,128)(2,1)S(1)}, u32[]{:S(2)}, u32[]{:S(2)}) async-start(bf16[128,4,1280]{0,2,1:T(8,128)(2,1)} %bitcast.12), calls=%async_computation.2 | async-start | bytes 2621440 | tf_op jit(solution)/shard_map/all_to_all | solution.py:29
  50.5 20.4 %collective-permute-start = (bf16[512,512]{1,0:T(8,128)(2,1)}, bf16[512,512]{1,0:T(8,128)(2,1)S(1)}, u32[]{:S(2)}, u32[]{:S(2)}) collective-permute-start(bf16[512,512]{1,0:T(8,128)(2,1)} %get-tuple-element.621), channel_id=1, source_target_pairs={{0,1},{1,2},{2,3},{3,4},{4,5},{5,6},{6,7},{7,8},{8,9},{9,10},{10,1... | collective-permute-start | bytes 1572872 | tf_op jit(solution)/shard_map/while/body/eval_jaxpr/ppermute | solution.py:18
  81.1 17.9 %collective-permute-start = (bf16[512,512]{1,0:T(8,128)(2,1)}, bf16[512,512]{1,0:T(8,128)(2,1)S(1)}, u32[]{:S(2)}, u32[]{:S(2)}) collective-permute-start(bf16[512,512]{1,0:T(8,128)(2,1)} %get-tuple-element.621), channel_id=1, source_target_pairs={{0,1},{1,2},{2,3},{3,4},{4,5},{5,6},{6,7},{7,8},{8,9},{9,10},{10,1... | collective-permute-start | bytes 1572872 | tf_op jit(solution)/shard_map/while/body/eval_jaxpr/ppermute | solution.py:18
  109.1 17.0 %collective-permute-start = (bf16[512,512]{1,0:T(8,128)(2,1)}, bf16[512,512]{1,0:T(8,128)(2,1)S(1)}, u32[]{:S(2)}, u32[]{:S(2)}) collective-permute-start(bf16[512,512]{1,0:T(8,128)(2,1)} %get-tuple-element.621), channel_id=1, source_target_pairs={{0,1},{1,2},{2,3},{3,4},{4,5},{5,6},{6,7},{7,8},{8,9},{9,10},{10,1... | collective-permute-start | bytes 1572872 | tf_op jit(solution)/shard_map/while/body/eval_jaxpr/ppermute | solution.py:18
  136.3 16.0 %collective-permute-start = (bf16[512,512]{1,0:T(8,128)(2,1)}, bf16[512,512]{1,0:T(8,128)(2,1)S(1)}, u32[]{:S(2)}, u32[]{:S(2)}) collective-permute-start(bf16[512,512]{1,0:T(8,128)(2,1)} %get-tuple-element.621), channel_id=1, source_target_pairs={{0,1},{1,2},{2,3},{3,4},{4,5},{5,6},{6,7},{7,8},{8,9},{9,10},{10,1... | collective-permute-start | bytes 1572872 | tf_op jit(solution)/shard_map/while/body/eval_jaxpr/ppermute | solution.py:18
  162.5 15.1 %collective-permute-start = (bf16[512,512]{1,0:T(8,128)(2,1)}, bf16[512,512]{1,0:T(8,128)(2,1)S(1)}, u32[]{:S(2)}, u32[]{:S(2)}) collective-permute-start(bf16[512,512]{1,0:T(8,128)(2,1)} %get-tuple-element.621), channel_id=1, source_target_pairs={{0,1},{1,2},{2,3},{3,4},{4,5},{5,6},{6,7},{7,8},{8,9},{9,10},{10,1... | collective-permute-start | bytes 1572872 | tf_op jit(solution)/shard_map/while/body/eval_jaxpr/ppermute | solution.py:18
  187.8 14.0 %collective-permute-start = (bf16[512,512]{1,0:T(8,128)(2,1)}, bf16[512,512]{1,0:T(8,128)(2,1)S(1)}, u32[]{:S(2)}, u32[]{:S(2)}) collective-permute-start(bf16[512,512]{1,0:T(8,128)(2,1)} %get-tuple-element.621), channel_id=1, source_target_pairs={{0,1},{1,2},{2,3},{3,4},{4,5},{5,6},{6,7},{7,8},{8,9},{9,10},{10,1... | collective-permute-start | bytes 1572872 | tf_op jit(solution)/shard_map/while/body/eval_jaxpr/ppermute | solution.py:18
  211.9 14.0 %collective-permute-start = (bf16[512,512]{1,0:T(8,128)(2,1)}, bf16[512,512]{1,0:T(8,128)(2,1)S(1)}, u32[]{:S(2)}, u32[]{:S(2)}) collective-permute-start(bf16[512,512]{1,0:T(8,128)(2,1)} %get-tuple-element.621), channel_id=1, source_target_pairs={{0,1},{1,2},{2,3},{3,4},{4,5},{5,6},{6,7},{7,8},{8,9},{9,10},{10,1... | collective-permute-start | bytes 1572872 | tf_op jit(solution)/shard_map/while/body/eval_jaxpr/ppermute | solution.py:18
  236.0 14.0 %collective-permute-start = (bf16[512,512]{1,0:T(8,128)(2,1)}, bf16[512,512]{1,0:T(8,128)(2,1)S(1)}, u32[]{:S(2)}, u32[]{:S(2)}) collective-permute-start(bf16[512,512]{1,0:T(8,128)(2,1)} %get-tuple-element.621), channel_id=1, source_target_pairs={{0,1},{1,2},{2,3},{3,4},{4,5},{5,6},{6,7},{7,8},{8,9},{9,10},{10,1... | collective-permute-start | bytes 1572872 | tf_op jit(solution)/shard_map/while/body/eval_jaxpr/ppermute | solution.py:18
  260.1 14.0 %collective-permute-start = (bf16[512,512]{1,0:T(8,128)(2,1)}, bf16[512,512]{1,0:T(8,128)(2,1)S(1)}, u32[]{:S(2)}, u32[]{:S(2)}) collective-permute-start(bf16[512,512]{1,0:T(8,128)(2,1)} %get-tuple-element.621), channel_id=1, source_target_pairs={{0,1},{1,2},{2,3},{3,4},{4,5},{5,6},{6,7},{7,8},{8,9},{9,10},{10,1... | collective-permute-start | bytes 1572872 | tf_op jit(solution)/shard_map/while/body/eval_jaxpr/ppermute | solution.py:18
  284.2 14.0 %collective-permute-start = (bf16[512,512]{1,0:T(8,128)(2,1)}, bf16[512,512]{1,0:T(8,128)(2,1)S(1)}, u32[]{:S(2)}, u32[]{:S(2)}) collective-permute-start(bf16[512,512]{1,0:T(8,128)(2,1)} %get-tuple-element.621), channel_id=1, source_target_pairs={{0,1},{1,2},{2,3},{3,4},{4,5},{5,6},{6,7},{7,8},{8,9},{9,10},{10,1... | collective-permute-start | bytes 1572872 | tf_op jit(solution)/shard_map/while/body/eval_jaxpr/ppermute | solution.py:18
  308.4 14.0 %collective-permute-start = (bf16[512,512]{1,0:T(8,128)(2,1)}, bf16[512,512]{1,0:T(8,128)(2,1)S(1)}, u32[]{:S(2)}, u32[]{:S(2)}) collective-permute-start(bf16[512,512]{1,0:T(8,128)(2,1)} %get-tuple-element.621), channel_id=1, source_target_pairs={{0,1},{1,2},{2,3},{3,4},{4,5},{5,6},{6,7},{7,8},{8,9},{9,10},{10,1... | collective-permute-start | bytes 1572872 | tf_op jit(solution)/shard_map/while/body/eval_jaxpr/ppermute | solution.py:18
  332.5 14.0 %collective-permute-start = (bf16[512,512]{1,0:T(8,128)(2,1)}, bf16[512,512]{1,0:T(8,128)(2,1)S(1)}, u32[]{:S(2)}, u32[]{:S(2)}) collective-permute-start(bf16[512,512]{1,0:T(8,128)(2,1)} %get-tuple-element.621), channel_id=1, source_target_pairs={{0,1},{1,2},{2,3},{3,4},{4,5},{5,6},{6,7},{7,8},{8,9},{9,10},{10,1... | collective-permute-start | bytes 1572872 | tf_op jit(solution)/shard_map/while/body/eval_jaxpr/ppermute | solution.py:18
  356.6 14.0 %collective-permute-start = (bf16[512,512]{1,0:T(8,128)(2,1)}, bf16[512,512]{1,0:T(8,128)(2,1)S(1)}, u32[]{:S(2)}, u32[]{:S(2)}) collective-permute-start(bf16[512,512]{1,0:T(8,128)(2,1)} %get-tuple-element.621), channel_id=1, source_target_pairs={{0,1},{1,2},{2,3},{3,4},{4,5},{5,6},{6,7},{7,8},{8,9},{9,10},{10,1... | collective-permute-start | bytes 1572872 | tf_op jit(solution)/shard_map/while/body/eval_jaxpr/ppermute | solution.py:18
  380.7 14.0 %collective-permute-start = (bf16[512,512]{1,0:T(8,128)(2,1)}, bf16[512,512]{1,0:T(8,128)(2,1)S(1)}, u32[]{:S(2)}, u32[]{:S(2)}) collective-permute-start(bf16[512,512]{1,0:T(8,128)(2,1)} %get-tuple-element.621), channel_id=1, source_target_pairs={{0,1},{1,2},{2,3},{3,4},{4,5},{5,6},{6,7},{7,8},{8,9},{9,10},{10,1... | collective-permute-start | bytes 1572872 | tf_op jit(solution)/shard_map/while/body/eval_jaxpr/ppermute | solution.py:18
  404.9 14.0 %collective-permute-start = (bf16[512,512]{1,0:T(8,128)(2,1)}, bf16[512,512]{1,0:T(8,128)(2,1)S(1)}, u32[]{:S(2)}, u32[]{:S(2)}) collective-permute-start(bf16[512,512]{1,0:T(8,128)(2,1)} %get-tuple-element.621), channel_id=1, source_target_pairs={{0,1},{1,2},{2,3},{3,4},{4,5},{5,6},{6,7},{7,8},{8,9},{9,10},{10,1... | collective-permute-start | bytes 1572872 | tf_op jit(solution)/shard_map/while/body/eval_jaxpr/ppermute | solution.py:18
  429.0 14.0 %collective-permute-start = (bf16[512,512]{1,0:T(8,128)(2,1)}, bf16[512,512]{1,0:T(8,128)(2,1)S(1)}, u32[]{:S(2)}, u32[]{:S(2)}) collective-permute-start(bf16[512,512]{1,0:T(8,128)(2,1)} %get-tuple-element.621), channel_id=1, source_target_pairs={{0,1},{1,2},{2,3},{3,4},{4,5},{5,6},{6,7},{7,8},{8,9},{9,10},{10,1... | collective-permute-start | bytes 1572872 | tf_op jit(solution)/shard_map/while/body/eval_jaxpr/ppermute | solution.py:18
  453.1 14.0 %collective-permute-start = (bf16[512,512]{1,0:T(8,128)(2,1)}, bf16[512,512]{1,0:T(8,128)(2,1)S(1)}, u32[]{:S(2)}, u32[]{:S(2)}) collective-permute-start(bf16[512,512]{1,0:T(8,128)(2,1)} %get-tuple-element.621), channel_id=1, source_target_pairs={{0,1},{1,2},{2,3},{3,4},{4,5},{5,6},{6,7},{7,8},{8,9},{9,10},{10,1... | collective-permute-start | bytes 1572872 | tf_op jit(solution)/shard_map/while/body/eval_jaxpr/ppermute | solution.py:18
  477.2 14.0 %collective-permute-start = (bf16[512,512]{1,0:T(8,128)(2,1)}, bf16[512,512]{1,0:T(8,128)(2,1)S(1)}, u32[]{:S(2)}, u32[]{:S(2)}) collective-permute-start(bf16[512,512]{1,0:T(8,128)(2,1)} %get-tuple-element.621), channel_id=1, source_target_pairs={{0,1},{1,2},{2,3},{3,4},{4,5},{5,6},{6,7},{7,8},{8,9},{9,10},{10,1... | collective-permute-start | bytes 1572872 | tf_op jit(solution)/shard_map/while/body/eval_jaxpr/ppermute | solution.py:18
  501.3 14.9 %collective-permute-start = (bf16[512,512]{1,0:T(8,128)(2,1)}, bf16[512,512]{1,0:T(8,128)(2,1)S(1)}, u32[]{:S(2)}, u32[]{:S(2)}) collective-permute-start(bf16[512,512]{1,0:T(8,128)(2,1)} %get-tuple-element.621), channel_id=1, source_target_pairs={{0,1},{1,2},{2,3},{3,4},{4,5},{5,6},{6,7},{7,8},{8,9},{9,10},{10,1... | collective-permute-start | bytes 1572872 | tf_op jit(solution)/shard_map/while/body/eval_jaxpr/ppermute | solution.py:18
  526.4 16.0 %collective-permute-start = (bf16[512,512]{1,0:T(8,128)(2,1)}, bf16[512,512]{1,0:T(8,128)(2,1)S(1)}, u32[]{:S(2)}, u32[]{:S(2)}) collective-permute-start(bf16[512,512]{1,0:T(8,128)(2,1)} %get-tuple-element.621), channel_id=1, source_target_pairs={{0,1},{1,2},{2,3},{3,4},{4,5},{5,6},{6,7},{7,8},{8,9},{9,10},{10,1... | collective-permute-start | bytes 1572872 | tf_op jit(solution)/shard_map/while/body/eval_jaxpr/ppermute | solution.py:18
  552.6 17.1 %collective-permute-start = (bf16[512,512]{1,0:T(8,128)(2,1)}, bf16[512,512]{1,0:T(8,128)(2,1)S(1)}, u32[]{:S(2)}, u32[]{:S(2)}) collective-permute-start(bf16[512,512]{1,0:T(8,128)(2,1)} %get-tuple-element.621), channel_id=1, source_target_pairs={{0,1},{1,2},{2,3},{3,4},{4,5},{5,6},{6,7},{7,8},{8,9},{9,10},{10,1... | collective-permute-start | bytes 1572872 | tf_op jit(solution)/shard_map/while/body/eval_jaxpr/ppermute | solution.py:18
  579.8 18.2 %collective-permute-start = (bf16[512,512]{1,0:T(8,128)(2,1)}, bf16[512,512]{1,0:T(8,128)(2,1)S(1)}, u32[]{:S(2)}, u32[]{:S(2)}) collective-permute-start(bf16[512,512]{1,0:T(8,128)(2,1)} %get-tuple-element.621), channel_id=1, source_target_pairs={{0,1},{1,2},{2,3},{3,4},{4,5},{5,6},{6,7},{7,8},{8,9},{9,10},{10,1... | collective-permute-start | bytes 1572872 | tf_op jit(solution)/shard_map/while/body/eval_jaxpr/ppermute | solution.py:18
  608.2 19.2 %collective-permute-start = (bf16[512,512]{1,0:T(8,128)(2,1)}, bf16[512,512]{1,0:T(8,128)(2,1)S(1)}, u32[]{:S(2)}, u32[]{:S(2)}) collective-permute-start(bf16[512,512]{1,0:T(8,128)(2,1)} %get-tuple-element.621), channel_id=1, source_target_pairs={{0,1},{1,2},{2,3},{3,4},{4,5},{5,6},{6,7},{7,8},{8,9},{9,10},{10,1... | collective-permute-start | bytes 1572872 | tf_op jit(solution)/shard_map/while/body/eval_jaxpr/ppermute | solution.py:18
  637.6 19.1 %collective-permute-start = (bf16[512,512]{1,0:T(8,128)(2,1)}, bf16[512,512]{1,0:T(8,128)(2,1)S(1)}, u32[]{:S(2)}, u32[]{:S(2)}) collective-permute-start(bf16[512,512]{1,0:T(8,128)(2,1)} %get-tuple-element.621), channel_id=1, source_target_pairs={{0,1},{1,2},{2,3},{3,4},{4,5},{5,6},{6,7},{7,8},{8,9},{9,10},{10,1... | collective-permute-start | bytes 1572872 | tf_op jit(solution)/shard_map/while/body/eval_jaxpr/ppermute | solution.py:18
  666.8 18.2 %collective-permute-start = (bf16[512,512]{1,0:T(8,128)(2,1)}, bf16[512,512]{1,0:T(8,128)(2,1)S(1)}, u32[]{:S(2)}, u32[]{:S(2)}) collective-permute-start(bf16[512,512]{1,0:T(8,128)(2,1)} %get-tuple-element.621), channel_id=1, source_target_pairs={{0,1},{1,2},{2,3},{3,4},{4,5},{5,6},{6,7},{7,8},{8,9},{9,10},{10,1... | collective-permute-start | bytes 1572872 | tf_op jit(solution)/shard_map/while/body/eval_jaxpr/ppermute | solution.py:18
  695.1 17.3 %collective-permute-start = (bf16[512,512]{1,0:T(8,128)(2,1)}, bf16[512,512]{1,0:T(8,128)(2,1)S(1)}, u32[]{:S(2)}, u32[]{:S(2)}) collective-permute-start(bf16[512,512]{1,0:T(8,128)(2,1)} %get-tuple-element.621), channel_id=1, source_target_pairs={{0,1},{1,2},{2,3},{3,4},{4,5},{5,6},{6,7},{7,8},{8,9},{9,10},{10,1... | collective-permute-start | bytes 1572872 | tf_op jit(solution)/shard_map/while/body/eval_jaxpr/ppermute | solution.py:18
  722.6 16.3 %collective-permute-start = (bf16[512,512]{1,0:T(8,128)(2,1)}, bf16[512,512]{1,0:T(8,128)(2,1)S(1)}, u32[]{:S(2)}, u32[]{:S(2)}) collective-permute-start(bf16[512,512]{1,0:T(8,128)(2,1)} %get-tuple-element.621), channel_id=1, source_target_pairs={{0,1},{1,2},{2,3},{3,4},{4,5},{5,6},{6,7},{7,8},{8,9},{9,10},{10,1... | collective-permute-start | bytes 1572872 | tf_op jit(solution)/shard_map/while/body/eval_jaxpr/ppermute | solution.py:18
  749.1 15.4 %collective-permute-start = (bf16[512,512]{1,0:T(8,128)(2,1)}, bf16[512,512]{1,0:T(8,128)(2,1)S(1)}, u32[]{:S(2)}, u32[]{:S(2)}) collective-permute-start(bf16[512,512]{1,0:T(8,128)(2,1)} %get-tuple-element.621), channel_id=1, source_target_pairs={{0,1},{1,2},{2,3},{3,4},{4,5},{5,6},{6,7},{7,8},{8,9},{9,10},{10,1... | collective-permute-start | bytes 1572872 | tf_op jit(solution)/shard_map/while/body/eval_jaxpr/ppermute | solution.py:18
  774.6 14.5 %collective-permute-start = (bf16[512,512]{1,0:T(8,128)(2,1)}, bf16[512,512]{1,0:T(8,128)(2,1)S(1)}, u32[]{:S(2)}, u32[]{:S(2)}) collective-permute-start(bf16[512,512]{1,0:T(8,128)(2,1)} %get-tuple-element.621), channel_id=1, source_target_pairs={{0,1},{1,2},{2,3},{3,4},{4,5},{5,6},{6,7},{7,8},{8,9},{9,10},{10,1... | collective-permute-start | bytes 1572872 | tf_op jit(solution)/shard_map/while/body/eval_jaxpr/ppermute | solution.py:18
  799.3 14.0 %collective-permute-start = (bf16[512,512]{1,0:T(8,128)(2,1)}, bf16[512,512]{1,0:T(8,128)(2,1)S(1)}, u32[]{:S(2)}, u32[]{:S(2)}) collective-permute-start(bf16[512,512]{1,0:T(8,128)(2,1)} %get-tuple-element.621), channel_id=1, source_target_pairs={{0,1},{1,2},{2,3},{3,4},{4,5},{5,6},{6,7},{7,8},{8,9},{9,10},{10,1... | collective-permute-start | bytes 1572872 | tf_op jit(solution)/shard_map/while/body/eval_jaxpr/ppermute | solution.py:18
  (4 other events, 53.1 us)
where the time goes:
time: 909 us; the launch traced here: 905 us
  waiting for transfers between devices  459 us (50%)
  local copies, waits for them, and re-layouts  194 us (21%)
  matrix products  109 us (12%)
  other arithmetic  66.8 us (7%)
  blocking collectives  59.4 us (7%)
  starting transfers between devices  14.6 us (2%)
    ppermute x31, waiting for transfers between devices, passed_along(): return lax.ppermute(value, axis, pairs)  441 us
    slice x64, local copies, waits for them, and re-layouts, attend(): value_tiles = tiles[:, :, width:].reshape(block_count, BLOCK, kv_local, DH)  89.5 us
    dot_general x32, matrix products, attend(): jnp.einsum('bqhgd,bkhd->bqhgk', query_tiles, key_tiles, preferred_element...  64.8 us
    all_to_all x1, blocking collectives, body(): lax.all_to_all(mixed, 'head', split_axis=0, concat_axis=1, tiled=True)  52.7 us
    dot_general x32, matrix products, attend(): jnp.einsum('bqhgk,bkhd->bqhgd', expo.astype(jnp.bfloat16), value_tiles, p...  44.2 us
    gather x32, local copies, waits for them, and re-layouts, attend(): tiles = piece.reshape(-1, BLOCK, 2 * width)[inner]  43 us
    slice x32, local copies, waits for them, and re-layouts, attend(): key_tiles = tiles[:, :, :width].reshape(block_count, BLOCK, kv_local, DH)  25.9 us
    while x62, local copies, waits for them, and re-layouts  24.6 us
  transfers between devices with their start and end apart: 34, of which 33 were waited for; matrix products, arithmetic and copies ran while one was open for 5% of the time, Pallas kernels for 0%

commit v1 on v0

v1 whole, which is shorter than its diff:
```python
import jax
import jax.numpy as jnp
from jax import lax
from jax.experimental import pallas as pl
from jax.experimental.pallas import tpu as pltpu
from jax.sharding import PartitionSpec as P

HQ = 40
HK = 8
DH = 128
BLOCK = 128
TOPK = 8
NSEG = 8
GROUP = HQ // HK
REMOTE = TOPK - 1
DEV = 128
ROWS = 16
PARTS = BLOCK // ROWS
UNITS = 2 * HK
MESSAGE = ROWS + 16
AXES = ("head", "ctx")
SCALE = DH**-0.5
LOG2E = 1.4426950408889634
FILL = -1e30


def remote_picks(sel_ref, me):
    picks = []
    passed = jnp.int32(0)
    for slot in range(REMOTE):
        passed = jnp.where(sel_ref[0, slot] == me, 1, passed)
        picks.append(jnp.where(passed == 1, sel_ref[0, slot + 1], sel_ref[0, slot]))
    return picks


def own_block():
    return lax.axis_index("head") * lax.axis_size("ctx") + lax.axis_index("ctx")


def pack_kernel(sel_ref, k_ref, v_ref, out_ref):
    picks = remote_picks(sel_ref, own_block())
    lane = lax.broadcasted_iota(jnp.int32, (16, BLOCK), 1)
    row = jnp.zeros((16, BLOCK), jnp.int32)
    for slot in range(REMOTE):
        row = jnp.where(lane == slot, picks[slot], row)
    row = row.astype(jnp.float32).astype(jnp.bfloat16)
    for unit in range(UNITS):
        src = k_ref if unit < HK else v_ref
        col = (unit % HK) * DH
        for part in range(PARTS):
            share = unit * PARTS + part
            out_ref[share, :ROWS, :] = src[part * ROWS : (part + 1) * ROWS, col : col + DH]
            out_ref[share, ROWS:, :] = row


def gather_kernel(picks_ref, table_ref, out_ref):
    @pl.loop(0, DEV)
    def _(dest):
        for slot in range(REMOTE):
            block = picks_ref[dest * REMOTE + slot]
            out_ref[dest, slot] = table_ref[block, :ROWS, :]


def attend_kernel(sel_ref, len_ref, q_ref, k_ref, v_ref, got_ref, out_ref, bias_ref):
    me = own_block()
    picks = remote_picks(sel_ref, me)
    row = lax.broadcasted_iota(jnp.int32, (BLOCK, BLOCK), 0) + me * BLOCK
    lane = lax.broadcasted_iota(jnp.int32, (BLOCK, BLOCK), 1)
    start = jnp.zeros((BLOCK, BLOCK), jnp.int32)
    end = jnp.int32(0)
    for seg in range(NSEG):
        end = end + len_ref[seg]
        start = jnp.where(row >= end, end, start)
    for slot, block in enumerate([me] + picks):
        pos = lane + block * BLOCK
        allowed = (pos <= row) & (pos >= start)
        bias_ref[:, slot * BLOCK : (slot + 1) * BLOCK] = jnp.where(allowed, 0.0, FILL)
    for head in range(HK):
        col = head * DH

        def stacked(own, unit):
            parts = [own[:, col : col + DH]]
            for slot in range(REMOTE):
                share = got_ref[unit * PARTS : (unit + 1) * PARTS, slot]
                parts.append(share.reshape(BLOCK, DH))
            return jnp.concatenate(parts, axis=0)

        keys = stacked(k_ref, head)
        vals = stacked(v_ref, HK + head)
        for g in range(GROUP):
            qcol = (head * GROUP + g) * DH
            q = q_ref[:, qcol : qcol + DH]
            s = lax.dot_general(q, keys, (((1,), (1,)), ((), ())), preferred_element_type=jnp.float32)
            s = s + bias_ref[...]
            top = jnp.max(s, axis=1, keepdims=True)
            p = jnp.exp2((s - top) * (SCALE * LOG2E))
            total = jnp.sum(p, axis=1, keepdims=True)
            mixed = jnp.dot(p.astype(jnp.bfloat16), vals, preferred_element_type=jnp.float32)
            out_ref[:, qcol : qcol + DH] = (mixed / total).astype(jnp.bfloat16)


def vmem():
    return pl.BlockSpec(memory_space=pltpu.VMEM)


def smem():
    return pl.BlockSpec(memory_space=pltpu.SMEM)


def params():
    return pltpu.CompilerParams(vmem_limit_bytes=48 * 1024 * 1024)


def body(queries, keys, values, selection, seg_lengths):
    packed = pl.pallas_call(
        pack_kernel,
        out_shape=jax.ShapeDtypeStruct((DEV, MESSAGE, DH), jnp.bfloat16),
        in_specs=[smem(), vmem(), vmem()],
        out_specs=vmem(),
        compiler_params=params(),
        name="pack",
    )(selection, keys, values)
    table = lax.all_to_all(packed, AXES, 0, 0, tiled=True)
    picks = table[:, ROWS, :REMOTE].astype(jnp.int32).reshape(DEV * REMOTE)
    shares = pl.pallas_call(
        gather_kernel,
        out_shape=jax.ShapeDtypeStruct((DEV, REMOTE, ROWS, DH), jnp.bfloat16),
        in_specs=[smem(), vmem()],
        out_specs=vmem(),
        compiler_params=params(),
        name="pick",
    )(picks, table)
    got = lax.all_to_all(shares, AXES, 0, 0, tiled=True)
    return pl.pallas_call(
        attend_kernel,
        out_shape=jax.ShapeDtypeStruct((BLOCK, HQ * DH), jnp.bfloat16),
        in_specs=[smem(), smem(), vmem(), vmem(), vmem(), vmem()],
        out_specs=vmem(),
        scratch_shapes=[pltpu.VMEM((BLOCK, TOPK * BLOCK), jnp.float32)],
        compiler_params=params(),
        name="attend",
    )(selection, seg_lengths, queries, keys, values, got)


def solution(mesh):
    return jax.shard_map(
        body,
        mesh=mesh,
        in_specs=(P(AXES, None), P(AXES, None), P(AXES, None), P(AXES, None), P()),
        out_specs=P(AXES, None),
        check_vma=False,
    )
```

time: 909 us -> 103 us (0.11)
  waiting for transfers between devices: 459 us -> 0 us
  local copies, waits for them, and re-layouts: 194 us -> 2.78 us
  matrix products: 109 us -> 0 us
  other arithmetic: 66.8 us -> 0.21 us
  blocking collectives: 59.4 us -> 81.1 us
  Pallas kernels: 0 us -> 18.5 us
  starting transfers between devices: 14.6 us -> 0 us
    ppermute x31 -> x0, waiting for transfers between devices: 441 us -> none  [passed_along(): return lax.ppermute(value, axis, pairs)]
    slice x96 -> x0, local copies, waits for them, and re-layouts: 115 us -> none  [the longest x64 89.5 us: attend(): value_tiles = tiles[:, :, width:].reshape(block_count, BLOCK, kv_local, DH)]
    dot_general x64 -> x0, matrix products: 109 us -> none  [the longest x32 64.8 us: attend(): jnp.einsum('bqhgd,bkhd->bqhgk', query_tiles, key_tiles, preferred_element...]
    reduce_sum x96 -> x0, other arithmetic: 49.5 us -> none  [the longest x32 23.8 us: attend(): total = total * shrink + jnp.sum(expo, axis=-1)]
    gather x32 -> x0, local copies, waits for them, and re-layouts: 43 us -> none  [attend(): tiles = piece.reshape(-1, BLOCK, 2 * width)[inner]]
    all_to_all x1 -> x2, blocking collectives: 52.7 us -> 81.1 us  [the longest x1 50.9 us: body(): got = lax.all_to_all(shares, AXES, 0, 0, tiled=True)]
    while x62 -> x0, local copies, waits for them, and re-layouts: 24.6 us -> none
    pallas_call x0 -> x3, Pallas kernels: none -> 18.5 us  [the longest x1 15.8 us: body(): pl.pallas_call(attend_kernel, out_shape=jax.ShapeDtypeStruct((BLOCK, HQ *...]
  transfers between devices with their start and end apart: 34 -> 0, of which waited for: 33 -> 0; matrix products, arithmetic and copies ran while one was open for 5% -> 0% of each run, Pallas kernels for 0% -> 0%
where the time goes in v1:
time: 103 us
  blocking collectives  81.1 us (79%)
  Pallas kernels  18.5 us (18%)
  local copies, waits for them, and re-layouts  2.78 us (3%)
    all_to_all x1, blocking collectives, body(): got = lax.all_to_all(shares, AXES, 0, 0, tiled=True)  50.9 us
    all_to_all x1, blocking collectives, body(): table = lax.all_to_all(packed, AXES, 0, 0, tiled=True)  30.2 us
    pallas_call x1, Pallas kernels, body(): pl.pallas_call(attend_kernel, out_shape=jax.ShapeDtypeStruct((BLOCK, HQ *...  15.8 us
    unnamed x16, local copies, waits for them, and re-layouts  2.59 us
    pallas_call x1, Pallas kernels, body(): pl.pallas_call(gather_kernel, out_shape=jax.ShapeDtypeStruct((DEV, REMOTE...  2.07 us

profile of v1, /device:TPU:1, one launch (start us, length us, event | category | flops | bytes accessed | tf_op | source)
XLA Modules:
  0.0 102.7 jit_solution(14429785069147384278)
XLA Ops:
  0.0 0.0 copy-start.1
  0.0 0.9 copy-done.1
  1.0 0.0 copy-start.3
  1.0 0.9 copy-done.3
  1.9 0.0 copy-start.5
  1.9 0.7 copy-done.5
  2.6 0.7 pack.1
  3.2 30.2 %all_to_all.10.table_ref = bf16[128,32,128]{2,1,0:T(8,128)(2,1)S(1)} all-to-all(bf16[128,32,128]{2,1,0:T(8,128)(2,1)S(1)} %pack.1), channel_id=1, replica_groups=mesh['head'=4,'ctx'=32] {'head','ctx'}, dimensions={0} | all-to-all | bytes 2097152 | tf_op jit(solution)/shard_map/all_to_all | solution.py:123
  33.4 0.2 fusion
  33.6 0.2 reshape.4.picks_ref
  33.8 2.1 %pick.1 = bf16[128,7,16,128]{3,2,1,0:T(8,128)(2,1)S(1)} custom-call(s32[896]{0:T(1024)S(1)} %reshape.4.picks_ref, bf16[128,32,128]{2,1,0:T(8,128)(2,1)S(1)} %all_to_all.10.table_ref), custom_call_target="tpu_custom_call" | custom-call | tf_op jit(solution)/shard_map/pick/pallas_call | solution.py:125
  35.9 0.0 copy-start
  35.9 0.0 copy-start.2
  36.0 0.0 copy-start.4
  36.0 0.0 copy-start.6
  36.0 0.0 copy-start.7
  36.0 50.9 %all_to_all.11.got_ref = bf16[128,7,16,128]{3,2,1,0:T(8,128)(2,1)S(1)} all-to-all(bf16[128,7,16,128]{3,2,1,0:T(8,128)(2,1)S(1)} %pick.1), channel_id=1, replica_groups=mesh['head'=4,'ctx'=32] {'head','ctx'}, dimensions={0} | all-to-all | bytes 7340032 | tf_op jit(solution)/shard_map/all_to_all | solution.py:133
  86.9 0.0 copy-done
  86.9 0.0 copy-done.2
  86.9 0.0 copy-done.4
  86.9 0.0 copy-done.6
  86.9 0.0 copy-done.7
  86.9 15.8 %attend.1 = bf16[128,5120]{1,0:T(8,128)(2,1)} custom-call(s32[1,8]{1,0:T(1,128)S(1)} %copy-done.6, s32[8]{0:T(128)S(1)} %copy-done.7, bf16[128,5120]{1,0:T(8,128)(2,1)S(1)} %copy-done, bf16[128,1024]{1,0:T(8,128)(2,1)S(1)} %copy-done.2, bf16[128,1024]{1,0:T(8,128)(2,1)S(1)} %copy-done.4, bf16[128,7,16,128]{3,2,1,0:T(8,128)(2,1)S(1)} %all_to_all.11.got_ref), custom_call_target="tpu_custom_call" | custom-call | tf_op jit(solution)/shard_map/attend/pallas_call | solution.py:134
Async XLA Ops:
  0.0 0.9 copy-start.1
  1.0 0.9 copy-start.3
  1.9 0.7 copy-start.5
  35.9 51.0 %copy-start = (bf16[128,5120]{1,0:T(8,128)(2,1)S(1)}, bf16[128,5120]{1,0:T(8,128)(2,1)}, u32[]{:S(2)}) copy-start(bf16[128,5120]{1,0:T(8,128)(2,1)} %q_ref.1) | copy-start | bytes 3932164
  35.9 51.0 %copy-start.2 = (bf16[128,1024]{1,0:T(8,128)(2,1)S(1)}, bf16[128,1024]{1,0:T(8,128)(2,1)}, u32[]{:S(2)}) copy-start(bf16[128,1024]{1,0:T(8,128)(2,1)} %k_ref.3) | copy-start | bytes 786436
  36.0 51.0 %copy-start.4 = (bf16[128,1024]{1,0:T(8,128)(2,1)S(1)}, bf16[128,1024]{1,0:T(8,128)(2,1)}, u32[]{:S(2)}) copy-start(bf16[128,1024]{1,0:T(8,128)(2,1)} %v_ref.3) | copy-start | bytes 786436
  36.0 51.0 %copy-start.6 = (s32[1,8]{1,0:T(1,128)S(1)}, s32[1,8]{1,0:T(1,128)}, u32[]{:S(2)}) copy-start(s32[1,8]{1,0:T(1,128)} %sel_ref.3) | copy-start | bytes 100
  36.0 51.0 %copy-start.7 = (s32[8]{0:T(128)S(1)}, s32[8]{0:T(128)}, u32[]{:S(2)}) copy-start(s32[8]{0:T(128)} %len_ref.1) | copy-start | bytes 100

commit v2 on v1

v2 whole, which is shorter than its diff:
```python
import jax
import jax.numpy as jnp
from jax import lax
from jax.experimental import pallas as pl
from jax.experimental.pallas import tpu as pltpu
from jax.sharding import PartitionSpec as P

HQ = 40
HK = 8
DH = 128
BLOCK = 128
TOPK = 8
NSEG = 8
GROUP = HQ // HK
REMOTE = TOPK - 1
DEV = 128
ROWS = 16
PARTS = BLOCK // ROWS
UNITS = 2 * HK
EXTRA = 8
MESSAGE = ROWS + EXTRA
AXES = ("head", "ctx")
SCALE = DH**-0.5
LOG2E = 1.4426950408889634
FILL = -1e30


def own_block():
    return lax.axis_index("head") * lax.axis_size("ctx") + lax.axis_index("ctx")


def remote_picks(sel_ref, me):
    picks = []
    passed = jnp.int32(0)
    for slot in range(REMOTE):
        passed = jnp.where(sel_ref[0, slot] == me, 1, passed)
        picks.append(jnp.where(passed == 1, sel_ref[0, slot + 1], sel_ref[0, slot]))
    return picks


def pack_kernel(sel_hbm, len_hbm, k_ref, v_ref, out_ref, bias_ref, sel_ref, len_ref, sems):
    scalars = [
        pltpu.make_async_copy(sel_hbm, sel_ref, sems.at[UNITS]),
        pltpu.make_async_copy(len_hbm, len_ref, sems.at[UNITS + 1]),
    ]
    shares = []
    for unit in range(UNITS):
        src = k_ref if unit < HK else v_ref
        col = (unit % HK) * DH
        shares.append(
            pltpu.make_async_copy(
                src.at[:, :, col : col + DH],
                out_ref.at[unit * PARTS : (unit + 1) * PARTS, :ROWS, :],
                sems.at[unit],
            )
        )
    for copy in scalars + shares:
        copy.start()
    for copy in scalars:
        copy.wait()
    me = own_block()
    picks = remote_picks(sel_ref, me)
    lane = lax.broadcasted_iota(jnp.int32, (EXTRA, BLOCK), 1)
    row = jnp.zeros((EXTRA, BLOCK), jnp.int32)
    for slot in range(REMOTE):
        row = jnp.where(lane == slot, picks[slot], row)
    row = row.astype(jnp.float32).astype(jnp.bfloat16)
    for share in range(DEV):
        out_ref[share, ROWS:, :] = row
    row = lax.broadcasted_iota(jnp.int32, (BLOCK, BLOCK), 0) + me * BLOCK
    lane = lax.broadcasted_iota(jnp.int32, (BLOCK, BLOCK), 1)
    start = jnp.zeros((BLOCK, BLOCK), jnp.int32)
    end = jnp.int32(0)
    for seg in range(NSEG):
        end = end + len_ref[seg]
        start = jnp.where(row >= end, end, start)
    for slot, block in enumerate([me] + picks):
        pos = lane + block * BLOCK
        allowed = (pos <= row) & (pos >= start)
        bias_ref[:, slot * BLOCK : (slot + 1) * BLOCK] = jnp.where(allowed, 0.0, FILL)
    for copy in shares:
        copy.wait()


def gather_kernel(picks_ref, table_ref, out_ref):
    @pl.loop(0, DEV, unroll=8)
    def _(dest):
        for slot in range(REMOTE):
            block = picks_ref[dest * REMOTE + slot]
            out_ref[dest, slot] = table_ref[block, :ROWS, :]


def attend_kernel(q_ref, k_ref, v_ref, bias_ref, got_ref, out_ref):
    for head in range(HK):
        col = head * DH

        def stacked(own, unit):
            parts = [own[:, col : col + DH]]
            for slot in range(REMOTE):
                share = got_ref[unit * PARTS : (unit + 1) * PARTS, slot]
                parts.append(share.reshape(BLOCK, DH))
            return jnp.concatenate(parts, axis=0)

        keys = stacked(k_ref, head)
        vals = stacked(v_ref, HK + head)
        ones = jnp.ones((TOPK * BLOCK, DH), jnp.bfloat16)
        vals = jnp.concatenate([vals, ones], axis=1)
        for g in range(GROUP):
            qcol = (head * GROUP + g) * DH
            q = q_ref[:, qcol : qcol + DH]
            s = lax.dot_general(q, keys, (((1,), (1,)), ((), ())), preferred_element_type=jnp.float32)
            s = s + bias_ref[...]
            top = jnp.max(s, axis=1, keepdims=True)
            p = jnp.exp2((s - top) * (SCALE * LOG2E)).astype(jnp.bfloat16)
            mixed = jnp.dot(p, vals, preferred_element_type=jnp.float32)
            out_ref[:, qcol : qcol + DH] = (mixed[:, :DH] / mixed[:, DH:]).astype(jnp.bfloat16)


def vmem():
    return pl.BlockSpec(memory_space=pltpu.VMEM)


def hbm():
    return pl.BlockSpec(memory_space=pltpu.HBM)


def smem():
    return pl.BlockSpec(memory_space=pltpu.SMEM)


def params():
    return pltpu.CompilerParams(vmem_limit_bytes=48 * 1024 * 1024)


def in_hbm(x):
    return pltpu.with_memory_space_constraint(x, pltpu.HBM)


def body(queries, keys, values, selection, seg_lengths):
    tiles = (PARTS, ROWS, HK * DH)
    packed, bias = pl.pallas_call(
        pack_kernel,
        out_shape=(
            jax.ShapeDtypeStruct((DEV, MESSAGE, DH), jnp.bfloat16),
            jax.ShapeDtypeStruct((BLOCK, TOPK * BLOCK), jnp.float32),
        ),
        in_specs=[hbm()] * 4,
        out_specs=(vmem(), vmem()),
        scratch_shapes=[
            pltpu.SMEM((1, TOPK), jnp.int32),
            pltpu.SMEM((NSEG,), jnp.int32),
            pltpu.SemaphoreType.DMA((UNITS + 2,)),
        ],
        compiler_params=params(),
        name="pack",
    )(in_hbm(selection), in_hbm(seg_lengths), in_hbm(keys.reshape(tiles)), in_hbm(values.reshape(tiles)))
    table = lax.all_to_all(packed, AXES, 0, 0, tiled=True)
    picks = table[:, ROWS, :REMOTE].astype(jnp.int32).reshape(DEV * REMOTE)
    shares = pl.pallas_call(
        gather_kernel,
        out_shape=jax.ShapeDtypeStruct((DEV, REMOTE, ROWS, DH), jnp.bfloat16),
        in_specs=[smem(), vmem()],
        out_specs=vmem(),
        compiler_params=params(),
        name="pick",
    )(picks, table)
    got = lax.all_to_all(shares, AXES, 0, 0, tiled=True)
    return pl.pallas_call(
        attend_kernel,
        out_shape=jax.ShapeDtypeStruct((BLOCK, HQ * DH), jnp.bfloat16),
        in_specs=[vmem()] * 5,
        out_specs=vmem(),
        compiler_params=params(),
        name="attend",
    )(queries, keys, values, bias, got)


def solution(mesh):
    return jax.shard_map(
        body,
        mesh=mesh,
        in_specs=(P(AXES, None), P(AXES, None), P(AXES, None), P(AXES, None), P()),
        out_specs=P(AXES, None),
        check_vma=False,
    )
```

time: 103 us -> 89.8 us (0.87)
  Pallas kernels: 18.5 us -> 10.5 us
  blocking collectives: 81.1 us -> 78.4 us
  local copies, waits for them, and re-layouts: 2.78 us -> 0.22 us
    pallas_call x1, Pallas kernels: 15.8 us -> 7.71 us  [body(): pl.pallas_call(attend_kernel, out_shape=jax.ShapeDtypeStruct((BLOCK, HQ *...]
    all_to_all x1, blocking collectives: 30.2 us -> 27.5 us  [body(): table = lax.all_to_all(packed, AXES, 0, 0, tiled=True)]
    unnamed x16 -> x6, local copies, waits for them, and re-layouts: 2.59 us -> 0.02 us
where the time goes in v2:
time: 89.8 us; the launch traced here: 89.4 us
  blocking collectives  78.4 us (87%)
  Pallas kernels  10.5 us (12%)
    all_to_all x1, blocking collectives, body(): got = lax.all_to_all(shares, AXES, 0, 0, tiled=True)  51 us
    all_to_all x1, blocking collectives, body(): table = lax.all_to_all(packed, AXES, 0, 0, tiled=True)  27.5 us
    pallas_call x1, Pallas kernels, body(): pl.pallas_call(attend_kernel, out_shape=jax.ShapeDtypeStruct((BLOCK, HQ *...  7.71 us

profile of v2, /device:TPU:1, one launch (start us, length us, event | category | flops | bytes accessed | tf_op | source)
XLA Modules:
  0.0 89.4 jit_solution(16171975233855700068)
XLA Ops:
  0.0 1.2 %pack.1 = (bf16[128,24,128]{2,1,0:T(8,128)(2,1)S(1)}, f32[128,1024]{1,0:T(8,128)S(1)}) custom-call(s32[1,8]{1,0:T(1,128)} %sel_hbm.1, s32[8]{0:T(128)} %len_hbm.1, bf16[8,16,1024]{2,1,0:T(8,128)(2,1)} %bitcast.2, bf16[8,16,1024]{2,1,0:T(8,128)(2,1)} %bitcast.3), custom_call_target="tpu_custom_call" | custom-call | tf_op jit(solution)/shard_map/pack/pallas_call | solution.py:141
  1.2 27.5 %all_to_all.10.table_ref = bf16[128,24,128]{2,1,0:T(8,128)(2,1)S(1)} all-to-all(bf16[128,24,128]{2,1,0:T(8,128)(2,1)S(1)} %get-tuple-element.8), channel_id=1, replica_groups=mesh['head'=4,'ctx'=32] {'head','ctx'}, dimensions={0} | all-to-all | bytes 1572864 | tf_op jit(solution)/shard_map/all_to_all | solution.py:157
  28.6 0.2 fusion
  28.9 0.2 reshape.12.picks_ref
  29.1 1.6 %pick.1 = bf16[128,7,16,128]{3,2,1,0:T(8,128)(2,1)S(1)} custom-call(s32[896]{0:T(1024)S(1)} %reshape.12.picks_ref, bf16[128,24,128]{2,1,0:T(8,128)(2,1)S(1)} %all_to_all.10.table_ref), custom_call_target="tpu_custom_call" | custom-call | tf_op jit(solution)/shard_map/pick/pallas_call | solution.py:159
  30.7 0.0 copy-start
  30.7 0.0 copy-start.1
  30.7 0.0 copy-start.2
  30.7 51.0 %all_to_all.11.got_ref = bf16[128,7,16,128]{3,2,1,0:T(8,128)(2,1)S(1)} all-to-all(bf16[128,7,16,128]{3,2,1,0:T(8,128)(2,1)S(1)} %pick.1), channel_id=1, replica_groups=mesh['head'=4,'ctx'=32] {'head','ctx'}, dimensions={0} | all-to-all | bytes 7340032 | tf_op jit(solution)/shard_map/all_to_all | solution.py:167
  81.7 0.0 copy-done
  81.7 0.0 copy-done.1
  81.7 0.0 copy-done.2
  81.7 7.7 %attend.1 = bf16[128,5120]{1,0:T(8,128)(2,1)} custom-call(bf16[128,5120]{1,0:T(8,128)(2,1)S(1)} %copy-done, bf16[128,1024]{1,0:T(8,128)(2,1)S(1)} %copy-done.1, bf16[128,1024]{1,0:T(8,128)(2,1)S(1)} %copy-done.2, f32[128,1024]{1,0:T(8,128)S(1)} %get-tuple-element.7.bias_ref, bf16[128,7,16,128]{3,2,1,0:T(8,128)(2,1)S(1)} %all_to_all.11.got_ref), custom_call_target="tpu_custom_call" | custom-call | tf_op jit(solution)/shard_map/attend/pallas_call | solution.py:168
Async XLA Ops:
  30.7 51.0 %copy-start = (bf16[128,5120]{1,0:T(8,128)(2,1)S(1)}, bf16[128,5120]{1,0:T(8,128)(2,1)}, u32[]{:S(2)}) copy-start(bf16[128,5120]{1,0:T(8,128)(2,1)} %q_ref.1) | copy-start | bytes 3932164
  30.7 51.0 %copy-start.1 = (bf16[128,1024]{1,0:T(8,128)(2,1)S(1)}, bf16[128,1024]{1,0:T(8,128)(2,1)}, u32[]{:S(2)}) copy-start(bf16[128,1024]{1,0:T(8,128)(2,1)} %k_ref.1) | copy-start | bytes 786436
  30.7 51.0 %copy-start.2 = (bf16[128,1024]{1,0:T(8,128)(2,1)S(1)}, bf16[128,1024]{1,0:T(8,128)(2,1)}, u32[]{:S(2)}) copy-start(bf16[128,1024]{1,0:T(8,128)(2,1)} %v_ref.1) | copy-start | bytes 786436

commit v3 on v2

--- a/solution.py
+++ b/solution.py
@@ -3,6 +3,7 @@
 from jax import lax
 from jax.experimental import pallas as pl
 from jax.experimental.pallas import tpu as pltpu
+from jax.sharding import Mesh
 from jax.sharding import PartitionSpec as P
 
 HQ = 40
@@ -17,16 +18,32 @@
 ROWS = 16
 PARTS = BLOCK // ROWS
 UNITS = 2 * HK
-EXTRA = 8
+EXTRA = 2
 MESSAGE = ROWS + EXTRA
-AXES = ("head", "ctx")
+AXES = ("y_lo", "core", "x", "y_hi", "z")
+SIZES = (2, 2, 4, 2, 4)
+ORDER = ("z", "x", "y_lo", "y_hi", "core")
 SCALE = DH**-0.5
 LOG2E = 1.4426950408889634
 FILL = -1e30
 
 
 def own_block():
-    return lax.axis_index("head") * lax.axis_size("ctx") + lax.axis_index("ctx")
+    block = jnp.int32(0)
+    for axis, size in zip(AXES, SIZES):
+        block = block * size + lax.axis_index(axis)
+    return block
+
+
+def place(block):
+    at = {}
+    for axis, size in zip(reversed(AXES), reversed(SIZES)):
+        at[axis] = block & (size - 1)
+        block = block >> (size.bit_length() - 1)
+    where = jnp.int32(0)
+    for axis in ORDER:
+        where = where * SIZES[AXES.index(axis)] + at[axis]
+    return where
 
 
 def remote_picks(sel_ref, me):
@@ -38,23 +55,16 @@
     return picks
 
 
-def pack_kernel(sel_hbm, len_hbm, k_ref, v_ref, out_ref, bias_ref, sel_ref, len_ref, sems):
+def pack_kernel(sel_hbm, len_hbm, k_hbm, v_hbm, out_ref, bias_ref, sel_ref, len_ref, k_ref, v_ref, sems):
     scalars = [
-        pltpu.make_async_copy(sel_hbm, sel_ref, sems.at[UNITS]),
-        pltpu.make_async_copy(len_hbm, len_ref, sems.at[UNITS + 1]),
+        pltpu.make_async_copy(sel_hbm, sel_ref, sems.at[0]),
+        pltpu.make_async_copy(len_hbm, len_ref, sems.at[1]),
     ]
-    shares = []
-    for unit in range(UNITS):
-        src = k_ref if unit < HK else v_ref
-        col = (unit % HK) * DH
-        shares.append(
-            pltpu.make_async_copy(
-                src.at[:, :, col : col + DH],
-                out_ref.at[unit * PARTS : (unit + 1) * PARTS, :ROWS, :],
-                sems.at[unit],
-            )
-        )
-    for copy in scalars + shares:
+    tokens = [
+        pltpu.make_async_copy(k_hbm, k_ref, sems.at[2]),
+        pltpu.make_async_copy(v_hbm, v_ref, sems.at[3]),
+    ]
+    for copy in scalars + tokens:
         copy.start()
     for copy in scalars:
         copy.wait()
@@ -63,10 +73,8 @@
     lane = lax.broadcasted_iota(jnp.int32, (EXTRA, BLOCK), 1)
     row = jnp.zeros((EXTRA, BLOCK), jnp.int32)
     for slot in range(REMOTE):
-        row = jnp.where(lane == slot, picks[slot], row)
-    row = row.astype(jnp.float32).astype(jnp.bfloat16)
-    for share in range(DEV):
-        out_ref[share, ROWS:, :] = row
+        row = jnp.where(lane == slot, place(picks[slot]), row)
+    extra = row.astype(jnp.float32).astype(jnp.bfloat16)
     row = lax.broadcasted_iota(jnp.int32, (BLOCK, BLOCK), 0) + me * BLOCK
     lane = lax.broadcasted_iota(jnp.int32, (BLOCK, BLOCK), 1)
     start = jnp.zeros((BLOCK, BLOCK), jnp.int32)
@@ -78,16 +86,26 @@
         pos = lane + block * BLOCK
         allowed = (pos <= row) & (pos >= start)
         bias_ref[:, slot * BLOCK : (slot + 1) * BLOCK] = jnp.where(allowed, 0.0, FILL)
-    for copy in shares:
+    for copy in tokens:
         copy.wait()
-
-
-def gather_kernel(picks_ref, table_ref, out_ref):
+    for unit in range(UNITS):
+        src = k_ref if unit < HK else v_ref
+        col = (unit % HK) * DH
+        for part in range(PARTS):
+            at = (unit * PARTS + part) * MESSAGE
+            out_ref[at : at + ROWS, :] = src[part * ROWS : (part + 1) * ROWS, col : col + DH]
+            out_ref[at + ROWS : at + MESSAGE, :] = extra
+
+
+def gather_kernel(picks_ref, table_ref, out_ref, share_ref):
+    for block in range(DEV):
+        share_ref[block] = table_ref[block * MESSAGE : block * MESSAGE + ROWS, :]
+
     @pl.loop(0, DEV, unroll=8)
     def _(dest):
         for slot in range(REMOTE):
             block = picks_ref[dest * REMOTE + slot]
-            out_ref[dest, slot] = table_ref[block, :ROWS, :]
+            out_ref[dest, slot] = share_ref[block]
 
 
 def attend_kernel(q_ref, k_ref, v_ref, bias_ref, got_ref, out_ref):
@@ -137,11 +155,10 @@
 
 
 def body(queries, keys, values, selection, seg_lengths):
-    tiles = (PARTS, ROWS, HK * DH)
     packed, bias = pl.pallas_call(
         pack_kernel,
         out_shape=(
-            jax.ShapeDtypeStruct((DEV, MESSAGE, DH), jnp.bfloat16),
+            jax.ShapeDtypeStruct((DEV * MESSAGE, DH), jnp.bfloat16),
             jax.ShapeDtypeStruct((BLOCK, TOPK * BLOCK), jnp.float32),
         ),
         in_specs=[hbm()] * 4,
@@ -149,22 +166,26 @@
         scratch_shapes=[
             pltpu.SMEM((1, TOPK), jnp.int32),
             pltpu.SMEM((NSEG,), jnp.int32),
-            pltpu.SemaphoreType.DMA((UNITS + 2,)),
+            pltpu.VMEM((BLOCK, HK * DH), jnp.bfloat16),
+            pltpu.VMEM((BLOCK, HK * DH), jnp.bfloat16),
+            pltpu.SemaphoreType.DMA((4,)),
         ],
         compiler_params=params(),
         name="pack",
-    )(in_hbm(selection), in_hbm(seg_lengths), in_hbm(keys.reshape(tiles)), in_hbm(values.reshape(tiles)))
-    table = lax.all_to_all(packed, AXES, 0, 0, tiled=True)
-    picks = table[:, ROWS, :REMOTE].astype(jnp.int32).reshape(DEV * REMOTE)
+    )(in_hbm(selection), in_hbm(seg_lengths), in_hbm(keys), in_hbm(values))
+    packed = packed.reshape(DEV, MESSAGE // EXTRA, EXTRA, DH)
+    table = lax.all_to_all(packed, ORDER, 0, 0, tiled=True)
+    picks = table[:, ROWS // EXTRA, 0, :REMOTE].astype(jnp.int32).reshape(DEV * REMOTE)
     shares = pl.pallas_call(
         gather_kernel,
         out_shape=jax.ShapeDtypeStruct((DEV, REMOTE, ROWS, DH), jnp.bfloat16),
         in_specs=[smem(), vmem()],
         out_specs=vmem(),
+        scratch_shapes=[pltpu.VMEM((DEV, ROWS, DH), jnp.bfloat16)],
         compiler_params=params(),
         name="pick",
-    )(picks, table)
-    got = lax.all_to_all(shares, AXES, 0, 0, tiled=True)
+    )(picks, table.reshape(DEV * MESSAGE, DH))
+    got = lax.all_to_all(shares, ORDER, 0, 0, tiled=True)
     return pl.pallas_call(
         attend_kernel,
         out_shape=jax.ShapeDtypeStruct((BLOCK, HQ * DH), jnp.bfloat16),
@@ -178,7 +199,7 @@
 def solution(mesh):
     return jax.shard_map(
         body,
-        mesh=mesh,
+        mesh=Mesh(mesh.devices.reshape(SIZES), AXES),
         in_specs=(P(AXES, None), P(AXES, None), P(AXES, None), P(AXES, None), P()),
         out_specs=P(AXES, None),
         check_vma=False,

time: 89.8 us -> 87.7 us (0.977)
  blocking collectives: 78.4 us -> 76.3 us
    all_to_all x2, blocking collectives: 78.4 us -> 76.3 us  [the longest x1 50.6 us: body(): got = lax.all_to_all(shares, ORDER, 0, 0, tiled=True)]
where the time goes in v3:
time: 87.7 us; the launch traced here: 87.5 us
  blocking collectives  76.3 us (87%)
  Pallas kernels  10.7 us (12%)
    all_to_all x1, blocking collectives, body(): got = lax.all_to_all(shares, ORDER, 0, 0, tiled=True)  50.6 us
    all_to_all x1, blocking collectives, body(): table = lax.all_to_all(packed, ORDER, 0, 0, tiled=True)  25.7 us
    pallas_call x1, Pallas kernels, body(): pl.pallas_call(attend_kernel, out_shape=jax.ShapeDtypeStruct((BLOCK, HQ *...  7.71 us
    pallas_call x1, Pallas kernels, body(): pl.pallas_call(gather_kernel, out_shape=jax.ShapeDtypeStruct((DEV, REMOTE...  1.78 us

profile of v3, /device:TPU:1, one launch (start us, length us, event | category | flops | bytes accessed | tf_op | source)
XLA Modules:
  0.0 87.5 jit_solution(6396608786853167136)
XLA Ops:
  0.0 1.2 %pack.1 = (bf16[2304,128]{1,0:T(8,128)(2,1)S(1)}, f32[128,1024]{1,0:T(8,128)S(1)}) custom-call(s32[1,8]{1,0:T(1,128)} %sel_hbm.1, s32[8]{0:T(128)} %len_hbm.1, bf16[128,1024]{1,0:T(8,128)(2,1)} %k_ref.1, bf16[128,1024]{1,0:T(8,128)(2,1)} %v_ref.1), custom_call_target="tpu_custom_call" | custom-call | tf_op jit(solution)/shard_map/pack/pallas_call | solution.py:158
  1.2 25.7 %all_to_all.10 = bf16[128,9,2,128]{3,2,1,0:T(2,128)(2,1)S(1)} all-to-all(bf16[128,9,2,128]{3,2,1,0:T(2,128)(2,1)S(1)} %bitcast.3), channel_id=1, replica_groups=mesh['y_lo'=2,'core'=2,'x'=4,'y_hi'=2,'z'=4] {'z','x','y_lo','y_hi','core'}, dimensions={0} | all-to-all | bytes 1179648 | tf_op jit(solution)/shard_map/all_to_all | solution.py:177
  27.0 0.2 fusion
  27.2 0.2 reshape.12.picks_ref
  27.4 1.8 %pick.1 = bf16[128,7,16,128]{3,2,1,0:T(8,128)(2,1)S(1)} custom-call(s32[896]{0:T(1024)S(1)} %reshape.12.picks_ref, bf16[2304,128]{1,0:T(8,128)(2,1)S(1)} %bitcast.2), custom_call_target="tpu_custom_call" | custom-call | tf_op jit(solution)/shard_map/pick/pallas_call | solution.py:179
  29.2 0.0 copy-start
  29.2 0.0 copy-start.1
  29.2 0.0 copy-start.2
  29.2 50.6 %all_to_all.11.got_ref = bf16[128,7,16,128]{3,2,1,0:T(8,128)(2,1)S(1)} all-to-all(bf16[128,7,16,128]{3,2,1,0:T(8,128)(2,1)S(1)} %pick.1), channel_id=1, replica_groups=mesh['y_lo'=2,'core'=2,'x'=4,'y_hi'=2,'z'=4] {'z','x','y_lo','y_hi','core'}, dimensions={0} | all-to-all | bytes 7340032 | tf_op jit(solution)/shard_map/all_to_all | solution.py:188
  79.8 0.0 copy-done
  79.8 0.0 copy-done.1
  79.8 0.0 copy-done.2
  79.8 7.7 %attend.1 = bf16[128,5120]{1,0:T(8,128)(2,1)} custom-call(bf16[128,5120]{1,0:T(8,128)(2,1)S(1)} %copy-done, bf16[128,1024]{1,0:T(8,128)(2,1)S(1)} %copy-done.1, bf16[128,1024]{1,0:T(8,128)(2,1)S(1)} %copy-done.2, f32[128,1024]{1,0:T(8,128)S(1)} %get-tuple-element.7.bias_ref, bf16[128,7,16,128]{3,2,1,0:T(8,128)(2,1)S(1)} %all_to_all.11.got_ref), custom_call_target="tpu_custom_call" | custom-call | tf_op jit(solution)/shard_map/attend/pallas_call | solution.py:189
Async XLA Ops:
  29.2 50.6 %copy-start = (bf16[128,5120]{1,0:T(8,128)(2,1)S(1)}, bf16[128,5120]{1,0:T(8,128)(2,1)}, u32[]{:S(2)}) copy-start(bf16[128,5120]{1,0:T(8,128)(2,1)} %q_ref.1) | copy-start | bytes 3932164
  29.2 50.6 %copy-start.1 = (bf16[128,1024]{1,0:T(8,128)(2,1)S(1)}, bf16[128,1024]{1,0:T(8,128)(2,1)}, u32[]{:S(2)}) copy-start(bf16[128,1024]{1,0:T(8,128)(2,1)} %k_ref.1) | copy-start | bytes 786436
  29.2 50.6 %copy-start.2 = (bf16[128,1024]{1,0:T(8,128)(2,1)S(1)}, bf16[128,1024]{1,0:T(8,128)(2,1)}, u32[]{:S(2)}) copy-start(bf16[128,1024]{1,0:T(8,128)(2,1)} %v_ref.1) | copy-start | bytes 786436

commit v4 on v3

--- a/solution.py
+++ b/solution.py
@@ -20,6 +20,7 @@
 UNITS = 2 * HK
 EXTRA = 2
 MESSAGE = ROWS + EXTRA
+SHARING = BLOCK // TOPK
 AXES = ("y_lo", "core", "x", "y_hi", "z")
 SIZES = (2, 2, 4, 2, 4)
 ORDER = ("z", "x", "y_lo", "y_hi", "core")
@@ -72,8 +73,9 @@
     picks = remote_picks(sel_ref, me)
     lane = lax.broadcasted_iota(jnp.int32, (EXTRA, BLOCK), 1)
     row = jnp.zeros((EXTRA, BLOCK), jnp.int32)
+    first = (place(me) & (SHARING - 1)) * TOPK
     for slot in range(REMOTE):
-        row = jnp.where(lane == slot, place(picks[slot]), row)
+        row = jnp.where(lane == first + slot, place(picks[slot]), row)
     extra = row.astype(jnp.float32).astype(jnp.bfloat16)
     row = lax.broadcasted_iota(jnp.int32, (BLOCK, BLOCK), 0) + me * BLOCK
     lane = lax.broadcasted_iota(jnp.int32, (BLOCK, BLOCK), 1)
@@ -97,18 +99,29 @@
             out_ref[at + ROWS : at + MESSAGE, :] = extra
 
 
-def gather_kernel(picks_ref, table_ref, out_ref, share_ref):
+def gather_kernel(table_ref, out_ref, share_ref, lanes_ref, picks_ref, sem):
+    for row in range(DEV // SHARING):
+        total = jnp.zeros((EXTRA, BLOCK), jnp.float32)
+        for block in range(row * SHARING, (row + 1) * SHARING):
+            at = block * MESSAGE + ROWS
+            total = total + table_ref[at : at + EXTRA, :].astype(jnp.float32)
+        lanes_ref[row : row + 1, :] = total[:1].astype(jnp.int32)
+    copy = pltpu.make_async_copy(lanes_ref, picks_ref, sem)
+    copy.start()
     for block in range(DEV):
         share_ref[block] = table_ref[block * MESSAGE : block * MESSAGE + ROWS, :]
-
-    @pl.loop(0, DEV, unroll=8)
-    def _(dest):
-        for slot in range(REMOTE):
-            block = picks_ref[dest * REMOTE + slot]
-            out_ref[dest, slot] = share_ref[block]
-
-
-def attend_kernel(q_ref, k_ref, v_ref, bias_ref, got_ref, out_ref):
+    copy.wait()
+
+    @pl.loop(0, DEV // SHARING)
+    def _(row):
+        for column in range(SHARING):
+            for slot in range(REMOTE):
+                block = picks_ref[row, column * TOPK + slot]
+                out_ref[row * SHARING + column, slot] = share_ref[block]
+
+
+def attend_kernel(q_ref, k_ref, v_ref, bias_ref, got_ref, out_hbm, out_ref, sems):
+    copies = []
     for head in range(HK):
         col = head * DH
 
@@ -132,6 +145,12 @@
             p = jnp.exp2((s - top) * (SCALE * LOG2E)).astype(jnp.bfloat16)
             mixed = jnp.dot(p, vals, preferred_element_type=jnp.float32)
             out_ref[:, qcol : qcol + DH] = (mixed[:, :DH] / mixed[:, DH:]).astype(jnp.bfloat16)
+        if head % 2 == 1:
+            cols = slice((head - 1) * GROUP * DH, (head + 1) * GROUP * DH)
+            copies.append(pltpu.make_async_copy(out_ref.at[:, cols], out_hbm.at[:, cols], sems.at[head // 2]))
+            copies[-1].start()
+    for copy in copies:
+        copy.wait()
 
 
 def vmem():
@@ -175,22 +194,30 @@
     )(in_hbm(selection), in_hbm(seg_lengths), in_hbm(keys), in_hbm(values))
     packed = packed.reshape(DEV, MESSAGE // EXTRA, EXTRA, DH)
     table = lax.all_to_all(packed, ORDER, 0, 0, tiled=True)
-    picks = table[:, ROWS // EXTRA, 0, :REMOTE].astype(jnp.int32).reshape(DEV * REMOTE)
     shares = pl.pallas_call(
         gather_kernel,
         out_shape=jax.ShapeDtypeStruct((DEV, REMOTE, ROWS, DH), jnp.bfloat16),
-        in_specs=[smem(), vmem()],
+        in_specs=[vmem()],
         out_specs=vmem(),
-        scratch_shapes=[pltpu.VMEM((DEV, ROWS, DH), jnp.bfloat16)],
+        scratch_shapes=[
+            pltpu.VMEM((DEV, ROWS, DH), jnp.bfloat16),
+            pltpu.VMEM((DEV // SHARING, BLOCK), jnp.int32),
+            pltpu.SMEM((DEV // SHARING, BLOCK), jnp.int32),
+            pltpu.SemaphoreType.DMA,
+        ],
         compiler_params=params(),
         name="pick",
-    )(picks, table.reshape(DEV * MESSAGE, DH))
+    )(table.reshape(DEV * MESSAGE, DH))
     got = lax.all_to_all(shares, ORDER, 0, 0, tiled=True)
     return pl.pallas_call(
         attend_kernel,
         out_shape=jax.ShapeDtypeStruct((BLOCK, HQ * DH), jnp.bfloat16),
         in_specs=[vmem()] * 5,
-        out_specs=vmem(),
+        out_specs=hbm(),
+        scratch_shapes=[
+            pltpu.VMEM((BLOCK, HQ * DH), jnp.bfloat16),
+            pltpu.SemaphoreType.DMA((HK // 2,)),
+        ],
         compiler_params=params(),
         name="attend",
     )(queries, keys, values, bias, got)

time: 87.7 us -> 86.9 us (level)
  no operation moved by 1% of the time
where the time goes in v4:
time: 86.9 us; the launch traced here: 86.7 us
  blocking collectives  76.3 us (88%)
  Pallas kernels  10.3 us (12%)
    all_to_all x1, blocking collectives, body(): got = lax.all_to_all(shares, ORDER, 0, 0, tiled=True)  50.6 us
    all_to_all x1, blocking collectives, body(): table = lax.all_to_all(packed, ORDER, 0, 0, tiled=True)  25.7 us
    pallas_call x1, Pallas kernels, body(): pl.pallas_call(attend_kernel, out_shape=jax.ShapeDtypeStruct((BLOCK, HQ *...  7.43 us

profile of v4, /device:TPU:1, one launch (start us, length us, event | category | flops | bytes accessed | tf_op | source)
XLA Modules:
  0.0 86.7 jit_solution(5654741204338710322)
XLA Ops:
  0.0 1.2 %pack.1 = (bf16[2304,128]{1,0:T(8,128)(2,1)S(1)}, f32[128,1024]{1,0:T(8,128)S(1)}) custom-call(s32[1,8]{1,0:T(1,128)} %sel_hbm.1, s32[8]{0:T(128)} %len_hbm.1, bf16[128,1024]{1,0:T(8,128)(2,1)} %k_ref.1, bf16[128,1024]{1,0:T(8,128)(2,1)} %v_ref.1), custom_call_target="tpu_custom_call" | custom-call | tf_op jit(solution)/shard_map/pack/pallas_call | solution.py:177
  1.2 25.7 %all_to_all.10 = bf16[128,9,2,128]{3,2,1,0:T(2,128)(2,1)S(1)} all-to-all(bf16[128,9,2,128]{3,2,1,0:T(2,128)(2,1)S(1)} %bitcast.3), channel_id=1, replica_groups=mesh['y_lo'=2,'core'=2,'x'=4,'y_hi'=2,'z'=4] {'z','x','y_lo','y_hi','core'}, dimensions={0} | all-to-all | bytes 1179648 | tf_op jit(solution)/shard_map/all_to_all | solution.py:196
  27.0 1.6 %pick.1 = bf16[128,7,16,128]{3,2,1,0:T(8,128)(2,1)S(1)} custom-call(bf16[2304,128]{1,0:T(8,128)(2,1)S(1)} %bitcast.2), custom_call_target="tpu_custom_call" | custom-call | tf_op jit(solution)/shard_map/pick/pallas_call | solution.py:197
  28.7 0.0 copy-start
  28.7 0.0 copy-start.1
  28.7 0.0 copy-start.2
  28.7 50.6 %all_to_all.11.got_ref = bf16[128,7,16,128]{3,2,1,0:T(8,128)(2,1)S(1)} all-to-all(bf16[128,7,16,128]{3,2,1,0:T(8,128)(2,1)S(1)} %pick.1), channel_id=1, replica_groups=mesh['y_lo'=2,'core'=2,'x'=4,'y_hi'=2,'z'=4] {'z','x','y_lo','y_hi','core'}, dimensions={0} | all-to-all | bytes 7340032 | tf_op jit(solution)/shard_map/all_to_all | solution.py:211
  79.3 0.0 copy-done
  79.3 0.0 copy-done.1
  79.3 0.0 copy-done.2
  79.3 7.4 %attend.1 = bf16[128,5120]{1,0:T(8,128)(2,1)} custom-call(bf16[128,5120]{1,0:T(8,128)(2,1)S(1)} %copy-done, bf16[128,1024]{1,0:T(8,128)(2,1)S(1)} %copy-done.1, bf16[128,1024]{1,0:T(8,128)(2,1)S(1)} %copy-done.2, f32[128,1024]{1,0:T(8,128)S(1)} %get-tuple-element.7.bias_ref, bf16[128,7,16,128]{3,2,1,0:T(8,128)(2,1)S(1)} %all_to_all.11.got_ref), custom_call_target="tpu_custom_call" | custom-call | tf_op jit(solution)/shard_map/attend/pallas_call | solution.py:212
Async XLA Ops:
  28.7 50.6 %copy-start = (bf16[128,5120]{1,0:T(8,128)(2,1)S(1)}, bf16[128,5120]{1,0:T(8,128)(2,1)}, u32[]{:S(2)}) copy-start(bf16[128,5120]{1,0:T(8,128)(2,1)} %q_ref.1) | copy-start | bytes 3932164
  28.7 50.6 %copy-start.1 = (bf16[128,1024]{1,0:T(8,128)(2,1)S(1)}, bf16[128,1024]{1,0:T(8,128)(2,1)}, u32[]{:S(2)}) copy-start(bf16[128,1024]{1,0:T(8,128)(2,1)} %k_ref.1) | copy-start | bytes 786436
  28.7 50.6 %copy-start.2 = (bf16[128,1024]{1,0:T(8,128)(2,1)S(1)}, bf16[128,1024]{1,0:T(8,128)(2,1)}, u32[]{:S(2)}) copy-start(bf16[128,1024]{1,0:T(8,128)(2,1)} %v_ref.1) | copy-start | bytes 786436

commit v5 on v4

--- a/solution.py
+++ b/solution.py
@@ -112,12 +112,12 @@
         share_ref[block] = table_ref[block * MESSAGE : block * MESSAGE + ROWS, :]
     copy.wait()
 
-    @pl.loop(0, DEV // SHARING)
-    def _(row):
-        for column in range(SHARING):
-            for slot in range(REMOTE):
-                block = picks_ref[row, column * TOPK + slot]
-                out_ref[row * SHARING + column, slot] = share_ref[block]
+    for dest in range(DEV):
+        row, first = dest // SHARING, dest % SHARING * TOPK
+        blocks = [picks_ref[row, first + slot] for slot in range(REMOTE)]
+        shares = [share_ref[block] for block in blocks]
+        for slot in range(REMOTE):
+            out_ref[dest, slot] = shares[slot]
 
 
 def attend_kernel(q_ref, k_ref, v_ref, bias_ref, got_ref, out_hbm, out_ref, sems):

time: 86.9 us -> 86.6 us (level)
  no operation moved by 1% of the time
where the time goes in v5:
time: 86.6 us; the launch traced here: 86.4 us
  blocking collectives  76.3 us (88%)
  Pallas kernels  10 us (12%)
    all_to_all x1, blocking collectives, body(): got = lax.all_to_all(shares, ORDER, 0, 0, tiled=True)  50.6 us
    all_to_all x1, blocking collectives, body(): table = lax.all_to_all(packed, ORDER, 0, 0, tiled=True)  25.7 us
    pallas_call x1, Pallas kernels, body(): pl.pallas_call(attend_kernel, out_shape=jax.ShapeDtypeStruct((BLOCK, HQ *...  7.43 us

profile of v5, /device:TPU:1, one launch (start us, length us, event | category | flops | bytes accessed | tf_op | source)
XLA Modules:
  0.0 86.4 jit_solution(17999765092911305745)
XLA Ops:
  0.0 1.2 %pack.1 = (bf16[2304,128]{1,0:T(8,128)(2,1)S(1)}, f32[128,1024]{1,0:T(8,128)S(1)}) custom-call(s32[1,8]{1,0:T(1,128)} %sel_hbm.1, s32[8]{0:T(128)} %len_hbm.1, bf16[128,1024]{1,0:T(8,128)(2,1)} %k_ref.1, bf16[128,1024]{1,0:T(8,128)(2,1)} %v_ref.1), custom_call_target="tpu_custom_call" | custom-call | tf_op jit(solution)/shard_map/pack/pallas_call | solution.py:177
  1.2 25.7 %all_to_all.10 = bf16[128,9,2,128]{3,2,1,0:T(2,128)(2,1)S(1)} all-to-all(bf16[128,9,2,128]{3,2,1,0:T(2,128)(2,1)S(1)} %bitcast.3), channel_id=1, replica_groups=mesh['y_lo'=2,'core'=2,'x'=4,'y_hi'=2,'z'=4] {'z','x','y_lo','y_hi','core'}, dimensions={0} | all-to-all | bytes 1179648 | tf_op jit(solution)/shard_map/all_to_all | solution.py:196
  27.0 1.4 %pick.1 = bf16[128,7,16,128]{3,2,1,0:T(8,128)(2,1)S(1)} custom-call(bf16[2304,128]{1,0:T(8,128)(2,1)S(1)} %bitcast.2), custom_call_target="tpu_custom_call" | custom-call | tf_op jit(solution)/shard_map/pick/pallas_call | solution.py:197
  28.4 0.0 copy-start
  28.4 0.0 copy-start.1
  28.4 0.0 copy-start.2
  28.4 50.6 %all_to_all.11.got_ref = bf16[128,7,16,128]{3,2,1,0:T(8,128)(2,1)S(1)} all-to-all(bf16[128,7,16,128]{3,2,1,0:T(8,128)(2,1)S(1)} %pick.1), channel_id=1, replica_groups=mesh['y_lo'=2,'core'=2,'x'=4,'y_hi'=2,'z'=4] {'z','x','y_lo','y_hi','core'}, dimensions={0} | all-to-all | bytes 7340032 | tf_op jit(solution)/shard_map/all_to_all | solution.py:211
  79.0 0.0 copy-done
  79.0 0.0 copy-done.1
  79.0 0.0 copy-done.2
  79.0 7.4 %attend.1 = bf16[128,5120]{1,0:T(8,128)(2,1)} custom-call(bf16[128,5120]{1,0:T(8,128)(2,1)S(1)} %copy-done, bf16[128,1024]{1,0:T(8,128)(2,1)S(1)} %copy-done.1, bf16[128,1024]{1,0:T(8,128)(2,1)S(1)} %copy-done.2, f32[128,1024]{1,0:T(8,128)S(1)} %get-tuple-element.7.bias_ref, bf16[128,7,16,128]{3,2,1,0:T(8,128)(2,1)S(1)} %all_to_all.11.got_ref), custom_call_target="tpu_custom_call" | custom-call | tf_op jit(solution)/shard_map/attend/pallas_call | solution.py:212
Async XLA Ops:
  28.4 50.6 %copy-start = (bf16[128,5120]{1,0:T(8,128)(2,1)S(1)}, bf16[128,5120]{1,0:T(8,128)(2,1)}, u32[]{:S(2)}) copy-start(bf16[128,5120]{1,0:T(8,128)(2,1)} %q_ref.1) | copy-start | bytes 3932164
  28.4 50.6 %copy-start.1 = (bf16[128,1024]{1,0:T(8,128)(2,1)S(1)}, bf16[128,1024]{1,0:T(8,128)(2,1)}, u32[]{:S(2)}) copy-start(bf16[128,1024]{1,0:T(8,128)(2,1)} %k_ref.1) | copy-start | bytes 786436
  28.4 50.6 %copy-start.2 = (bf16[128,1024]{1,0:T(8,128)(2,1)S(1)}, bf16[128,1024]{1,0:T(8,128)(2,1)}, u32[]{:S(2)}) copy-start(bf16[128,1024]{1,0:T(8,128)(2,1)} %v_ref.1) | copy-start | bytes 786436

commit v6 on v5

--- a/solution.py
+++ b/solution.py
@@ -56,7 +56,7 @@
     return picks
 
 
-def pack_kernel(sel_hbm, len_hbm, k_hbm, v_hbm, out_ref, bias_ref, sel_ref, len_ref, k_ref, v_ref, sems):
+def pack_kernel(sel_hbm, len_hbm, k_hbm, v_hbm, out_ref, bias_ref, turned_ref, sel_ref, len_ref, k_ref, v_ref, sems):
     scalars = [
         pltpu.make_async_copy(sel_hbm, sel_ref, sems.at[0]),
         pltpu.make_async_copy(len_hbm, len_ref, sems.at[1]),
@@ -87,15 +87,19 @@
     for slot, block in enumerate([me] + picks):
         pos = lane + block * BLOCK
         allowed = (pos <= row) & (pos >= start)
-        bias_ref[:, slot * BLOCK : (slot + 1) * BLOCK] = jnp.where(allowed, 0.0, FILL)
+        bias_ref[:, slot * BLOCK : (slot + 1) * BLOCK] = jnp.where(allowed, 0.0, FILL).astype(jnp.bfloat16)
     for copy in tokens:
         copy.wait()
     for unit in range(UNITS):
-        src = k_ref if unit < HK else v_ref
         col = (unit % HK) * DH
+        if unit < HK:
+            tile = k_ref[:, col : col + DH].T
+            turned_ref[col : col + DH, :] = tile
+        else:
+            tile = v_ref[:, col : col + DH]
         for part in range(PARTS):
             at = (unit * PARTS + part) * MESSAGE
-            out_ref[at : at + ROWS, :] = src[part * ROWS : (part + 1) * ROWS, col : col + DH]
+            out_ref[at : at + ROWS, :] = tile[part * ROWS : (part + 1) * ROWS, :]
             out_ref[at + ROWS : at + MESSAGE, :] = extra
 
 
@@ -120,35 +124,47 @@
             out_ref[dest, slot] = shares[slot]
 
 
-def attend_kernel(q_ref, k_ref, v_ref, bias_ref, got_ref, out_hbm, out_ref, sems):
+def attend_kernel(q_ref, turned_ref, v_ref, bias_ref, got_ref, out_hbm, out_ref, sems):
     copies = []
-    for head in range(HK):
-        col = head * DH
-
-        def stacked(own, unit):
-            parts = [own[:, col : col + DH]]
-            for slot in range(REMOTE):
-                share = got_ref[unit * PARTS : (unit + 1) * PARTS, slot]
-                parts.append(share.reshape(BLOCK, DH))
-            return jnp.concatenate(parts, axis=0)
-
-        keys = stacked(k_ref, head)
-        vals = stacked(v_ref, HK + head)
-        ones = jnp.ones((TOPK * BLOCK, DH), jnp.bfloat16)
-        vals = jnp.concatenate([vals, ones], axis=1)
-        for g in range(GROUP):
-            qcol = (head * GROUP + g) * DH
-            q = q_ref[:, qcol : qcol + DH]
-            s = lax.dot_general(q, keys, (((1,), (1,)), ((), ())), preferred_element_type=jnp.float32)
-            s = s + bias_ref[...]
-            top = jnp.max(s, axis=1, keepdims=True)
-            p = jnp.exp2((s - top) * (SCALE * LOG2E)).astype(jnp.bfloat16)
-            mixed = jnp.dot(p, vals, preferred_element_type=jnp.float32)
-            out_ref[:, qcol : qcol + DH] = (mixed[:, :DH] / mixed[:, DH:]).astype(jnp.bfloat16)
-        if head % 2 == 1:
-            cols = slice((head - 1) * GROUP * DH, (head + 1) * GROUP * DH)
-            copies.append(pltpu.make_async_copy(out_ref.at[:, cols], out_hbm.at[:, cols], sems.at[head // 2]))
+    row = lax.broadcasted_iota(jnp.int32, (BLOCK, BLOCK), 0)
+    lane = lax.broadcasted_iota(jnp.int32, (BLOCK, BLOCK), 1)
+    identity = jnp.where(row == lane, 1.0, 0.0).astype(jnp.bfloat16)
+    ones = jnp.ones((TOPK * BLOCK, DH), jnp.bfloat16)
+
+    def remote(unit):
+        return [got_ref[unit * PARTS : (unit + 1) * PARTS, slot].reshape(BLOCK, DH) for slot in range(REMOTE)]
+
+    def operands(head):
+        own = slice(head * DH, (head + 1) * DH)
+        keys = jnp.concatenate([turned_ref[own, :]] + remote(head), axis=1)
+        vals = jnp.concatenate([v_ref[:, own]] + remote(HK + head), axis=0)
+        return jnp.concatenate([keys, bias_ref[...]], axis=0), jnp.concatenate([vals, ones], axis=1)
+
+    def scores(index, keys):
+        q = jnp.concatenate([q_ref[:, index * DH : (index + 1) * DH], identity], axis=1)
+        return jnp.dot(q, keys, preferred_element_type=jnp.float32)
+
+    def finish(index, p, vals):
+        mixed = jnp.dot(p, vals, preferred_element_type=jnp.float32)
+        out_ref[:, index * DH : (index + 1) * DH] = (mixed[:, :DH] / mixed[:, DH:]).astype(jnp.bfloat16)
+        if (index + 1) % (2 * GROUP) == 0:
+            cols = slice((index + 1 - 2 * GROUP) * DH, (index + 1) * DH)
+            sem = sems.at[index // (2 * GROUP)]
+            copies.append(pltpu.make_async_copy(out_ref.at[:, cols], out_hbm.at[:, cols], sem))
             copies[-1].start()
+
+    pairs = [operands(head) for head in range(HK)]
+    s = scores(0, pairs[0][0])
+    before = None
+    for index in range(HQ):
+        later = scores(index + 1, pairs[(index + 1) // GROUP][0]) if index + 1 < HQ else None
+        top = jnp.max(s, axis=1, keepdims=True)
+        p = jnp.exp2((s - top) * (SCALE * LOG2E)).astype(jnp.bfloat16)
+        if before is not None:
+            finish(*before)
+        before = (index, p, pairs[index // GROUP][1])
+        s = later
+    finish(*before)
     for copy in copies:
         copy.wait()
 
@@ -174,14 +190,15 @@
 
 
 def body(queries, keys, values, selection, seg_lengths):
-    packed, bias = pl.pallas_call(
+    packed, bias, turned = pl.pallas_call(
         pack_kernel,
         out_shape=(
             jax.ShapeDtypeStruct((DEV * MESSAGE, DH), jnp.bfloat16),
-            jax.ShapeDtypeStruct((BLOCK, TOPK * BLOCK), jnp.float32),
+            jax.ShapeDtypeStruct((BLOCK, TOPK * BLOCK), jnp.bfloat16),
+            jax.ShapeDtypeStruct((HK * DH, BLOCK), jnp.bfloat16),
         ),
         in_specs=[hbm()] * 4,
-        out_specs=(vmem(), vmem()),
+        out_specs=(vmem(), vmem(), vmem()),
         scratch_shapes=[
             pltpu.SMEM((1, TOPK), jnp.int32),
             pltpu.SMEM((NSEG,), jnp.int32),
@@ -220,7 +237,7 @@
         ],
         compiler_params=params(),
         name="attend",
-    )(queries, keys, values, bias, got)
+    )(queries, turned, values, bias, got)
 
 
 def solution(mesh):

time: 86.6 us -> 86.3 us (level)
  no operation moved by 1% of the time
where the time goes in v6:
time: 86.3 us; the launch traced here: 86.1 us
  blocking collectives  76.3 us (88%)
  Pallas kernels  9.79 us (11%)
    all_to_all x1, blocking collectives, body(): got = lax.all_to_all(shares, ORDER, 0, 0, tiled=True)  50.6 us
    all_to_all x1, blocking collectives, body(): table = lax.all_to_all(packed, ORDER, 0, 0, tiled=True)  25.7 us
    pallas_call x1, Pallas kernels, body(): pl.pallas_call(attend_kernel, out_shape=jax.ShapeDtypeStruct((BLOCK, HQ *...  7.16 us

profile of v6, /device:TPU:1, one launch (start us, length us, event | category | flops | bytes accessed | tf_op | source)
XLA Modules:
  0.0 86.1 jit_solution(8864946576363611119)
XLA Ops:
  0.0 1.3 %pack.1 = (bf16[2304,128]{1,0:T(8,128)(2,1)S(1)}, bf16[128,1024]{1,0:T(8,128)(2,1)S(1)}, bf16[1024,128]{1,0:T(8,128)(2,1)S(1)}) custom-call(s32[1,8]{1,0:T(1,128)} %sel_hbm.1, s32[8]{0:T(128)} %len_hbm.1, bf16[128,1024]{1,0:T(8,128)(2,1)} %k_hbm.1, bf16[128,1024]{1,0:T(8,128)(2,1)} %v_ref.1), custom_call_target="tpu_custom_call" | custom-call | tf_op jit(solution)/shard_map/pack/pallas_call | solution.py:193
  1.3 25.7 %all_to_all.10 = bf16[128,9,2,128]{3,2,1,0:T(2,128)(2,1)S(1)} all-to-all(bf16[128,9,2,128]{3,2,1,0:T(2,128)(2,1)S(1)} %bitcast.3), channel_id=1, replica_groups=mesh['y_lo'=2,'core'=2,'x'=4,'y_hi'=2,'z'=4] {'z','x','y_lo','y_hi','core'}, dimensions={0} | all-to-all | bytes 1179648 | tf_op jit(solution)/shard_map/all_to_all | solution.py:213
  27.0 1.4 %pick.1 = bf16[128,7,16,128]{3,2,1,0:T(8,128)(2,1)S(1)} custom-call(bf16[2304,128]{1,0:T(8,128)(2,1)S(1)} %bitcast.2), custom_call_target="tpu_custom_call" | custom-call | tf_op jit(solution)/shard_map/pick/pallas_call | solution.py:214
  28.4 0.0 copy-start
  28.4 0.0 copy-start.1
  28.4 50.6 %all_to_all.11.got_ref = bf16[128,7,16,128]{3,2,1,0:T(8,128)(2,1)S(1)} all-to-all(bf16[128,7,16,128]{3,2,1,0:T(8,128)(2,1)S(1)} %pick.1), channel_id=1, replica_groups=mesh['y_lo'=2,'core'=2,'x'=4,'y_hi'=2,'z'=4] {'z','x','y_lo','y_hi','core'}, dimensions={0} | all-to-all | bytes 7340032 | tf_op jit(solution)/shard_map/all_to_all | solution.py:228
  79.0 0.0 copy-done
  79.0 0.0 copy-done.1
  79.0 7.2 %attend.1 = bf16[128,5120]{1,0:T(8,128)(2,1)} custom-call(bf16[128,5120]{1,0:T(8,128)(2,1)S(1)} %copy-done, bf16[1024,128]{1,0:T(8,128)(2,1)S(1)} %get-tuple-element.8.turned_ref, bf16[128,1024]{1,0:T(8,128)(2,1)S(1)} %copy-done.1, bf16[128,1024]{1,0:T(8,128)(2,1)S(1)} %get-tuple-element.9.bias_ref, bf16[128,7,16,128]{3,2,1,0:T(8,128)(2,1)S(1)} %all_to_all.11.got_ref), custom_call_target="tpu_custom_call" | custom-call | tf_op jit(solution)/shard_map/attend/pallas_call | solution.py:229
Async XLA Ops:
  28.4 50.6 %copy-start = (bf16[128,5120]{1,0:T(8,128)(2,1)S(1)}, bf16[128,5120]{1,0:T(8,128)(2,1)}, u32[]{:S(2)}) copy-start(bf16[128,5120]{1,0:T(8,128)(2,1)} %q_ref.1) | copy-start | bytes 3932164
  28.4 50.6 %copy-start.1 = (bf16[128,1024]{1,0:T(8,128)(2,1)S(1)}, bf16[128,1024]{1,0:T(8,128)(2,1)}, u32[]{:S(2)}) copy-start(bf16[128,1024]{1,0:T(8,128)(2,1)} %v_ref.1) | copy-start | bytes 786436

commit v7 on v6

--- a/solution.py
+++ b/solution.py
@@ -88,9 +88,9 @@
         pos = lane + block * BLOCK
         allowed = (pos <= row) & (pos >= start)
         bias_ref[:, slot * BLOCK : (slot + 1) * BLOCK] = jnp.where(allowed, 0.0, FILL).astype(jnp.bfloat16)
-    for copy in tokens:
-        copy.wait()
     for unit in range(UNITS):
+        if unit % HK == 0:
+            tokens[unit // HK].wait()
         col = (unit % HK) * DH
         if unit < HK:
             tile = k_ref[:, col : col + DH].T
@@ -126,6 +126,7 @@
 
 def attend_kernel(q_ref, turned_ref, v_ref, bias_ref, got_ref, out_hbm, out_ref, sems):
     copies = []
+    ends = [16, 28, 36, HQ]
     row = lax.broadcasted_iota(jnp.int32, (BLOCK, BLOCK), 0)
     lane = lax.broadcasted_iota(jnp.int32, (BLOCK, BLOCK), 1)
     identity = jnp.where(row == lane, 1.0, 0.0).astype(jnp.bfloat16)
@@ -147,10 +148,10 @@
     def finish(index, p, vals):
         mixed = jnp.dot(p, vals, preferred_element_type=jnp.float32)
         out_ref[:, index * DH : (index + 1) * DH] = (mixed[:, :DH] / mixed[:, DH:]).astype(jnp.bfloat16)
-        if (index + 1) % (2 * GROUP) == 0:
-            cols = slice((index + 1 - 2 * GROUP) * DH, (index + 1) * DH)
-            sem = sems.at[index // (2 * GROUP)]
-            copies.append(pltpu.make_async_copy(out_ref.at[:, cols], out_hbm.at[:, cols], sem))
+        if index + 1 in ends:
+            part = ends.index(index + 1)
+            cols = slice(ends[part - 1] * DH if part else 0, (index + 1) * DH)
+            copies.append(pltpu.make_async_copy(out_ref.at[:, cols], out_hbm.at[:, cols], sems.at[part]))
             copies[-1].start()
 
     pairs = [operands(head) for head in range(HK)]

time: 86.3 us -> 86.2 us (level)
  no operation moved by 1% of the time
where the time goes in v7:
time: 86.2 us; the launch traced here: 86 us
  blocking collectives  76.3 us (89%)
  Pallas kernels  9.68 us (11%)
    all_to_all x1, blocking collectives, body(): got = lax.all_to_all(shares, ORDER, 0, 0, tiled=True)  50.6 us
    all_to_all x1, blocking collectives, body(): table = lax.all_to_all(packed, ORDER, 0, 0, tiled=True)  25.7 us
    pallas_call x1, Pallas kernels, body(): pl.pallas_call(attend_kernel, out_shape=jax.ShapeDtypeStruct((BLOCK, HQ *...  7.09 us

profile of v7, /device:TPU:1, one launch (start us, length us, event | category | flops | bytes accessed | tf_op | source)
XLA Modules:
  0.0 86.0 jit_solution(10041728420304557603)
XLA Ops:
  0.0 1.2 %pack.1 = (bf16[2304,128]{1,0:T(8,128)(2,1)S(1)}, bf16[128,1024]{1,0:T(8,128)(2,1)S(1)}, bf16[1024,128]{1,0:T(8,128)(2,1)S(1)}) custom-call(s32[1,8]{1,0:T(1,128)} %sel_hbm.1, s32[8]{0:T(128)} %len_hbm.1, bf16[128,1024]{1,0:T(8,128)(2,1)} %k_hbm.1, bf16[128,1024]{1,0:T(8,128)(2,1)} %v_ref.1), custom_call_target="tpu_custom_call" | custom-call | tf_op jit(solution)/shard_map/pack/pallas_call | solution.py:194
  1.2 25.7 %all_to_all.10 = bf16[128,9,2,128]{3,2,1,0:T(2,128)(2,1)S(1)} all-to-all(bf16[128,9,2,128]{3,2,1,0:T(2,128)(2,1)S(1)} %bitcast.3), channel_id=1, replica_groups=mesh['y_lo'=2,'core'=2,'x'=4,'y_hi'=2,'z'=4] {'z','x','y_lo','y_hi','core'}, dimensions={0} | all-to-all | bytes 1179648 | tf_op jit(solution)/shard_map/all_to_all | solution.py:214
  27.0 1.4 %pick.1 = bf16[128,7,16,128]{3,2,1,0:T(8,128)(2,1)S(1)} custom-call(bf16[2304,128]{1,0:T(8,128)(2,1)S(1)} %bitcast.2), custom_call_target="tpu_custom_call" | custom-call | tf_op jit(solution)/shard_map/pick/pallas_call | solution.py:215
  28.4 0.0 copy-start
  28.4 0.0 copy-start.1
  28.4 50.6 %all_to_all.11.got_ref = bf16[128,7,16,128]{3,2,1,0:T(8,128)(2,1)S(1)} all-to-all(bf16[128,7,16,128]{3,2,1,0:T(8,128)(2,1)S(1)} %pick.1), channel_id=1, replica_groups=mesh['y_lo'=2,'core'=2,'x'=4,'y_hi'=2,'z'=4] {'z','x','y_lo','y_hi','core'}, dimensions={0} | all-to-all | bytes 7340032 | tf_op jit(solution)/shard_map/all_to_all | solution.py:229
  78.9 0.0 copy-done
  78.9 0.0 copy-done.1
  78.9 7.1 %attend.1 = bf16[128,5120]{1,0:T(8,128)(2,1)} custom-call(bf16[128,5120]{1,0:T(8,128)(2,1)S(1)} %copy-done, bf16[1024,128]{1,0:T(8,128)(2,1)S(1)} %get-tuple-element.8.turned_ref, bf16[128,1024]{1,0:T(8,128)(2,1)S(1)} %copy-done.1, bf16[128,1024]{1,0:T(8,128)(2,1)S(1)} %get-tuple-element.9.bias_ref, bf16[128,7,16,128]{3,2,1,0:T(8,128)(2,1)S(1)} %all_to_all.11.got_ref), custom_call_target="tpu_custom_call" | custom-call | tf_op jit(solution)/shard_map/attend/pallas_call | solution.py:230
Async XLA Ops:
  28.4 50.6 %copy-start = (bf16[128,5120]{1,0:T(8,128)(2,1)S(1)}, bf16[128,5120]{1,0:T(8,128)(2,1)}, u32[]{:S(2)}) copy-start(bf16[128,5120]{1,0:T(8,128)(2,1)} %q_ref.1) | copy-start | bytes 3932164
  28.4 50.6 %copy-start.1 = (bf16[128,1024]{1,0:T(8,128)(2,1)S(1)}, bf16[128,1024]{1,0:T(8,128)(2,1)}, u32[]{:S(2)}) copy-start(bf16[128,1024]{1,0:T(8,128)(2,1)} %v_ref.1) | copy-start | bytes 786436

commit v8 on v7

--- a/solution.py
+++ b/solution.py
@@ -154,17 +154,19 @@
             copies.append(pltpu.make_async_copy(out_ref.at[:, cols], out_hbm.at[:, cols], sems.at[part]))
             copies[-1].start()
 
-    pairs = [operands(head) for head in range(HK)]
-    s = scores(0, pairs[0][0])
+    pair = after = operands(0)
+    s = scores(0, pair[0])
     before = None
     for index in range(HQ):
-        later = scores(index + 1, pairs[(index + 1) // GROUP][0]) if index + 1 < HQ else None
+        if (index + 1) % GROUP == 0 and index + 1 < HQ:
+            after = operands((index + 1) // GROUP)
+        later = scores(index + 1, after[0]) if index + 1 < HQ else None
         top = jnp.max(s, axis=1, keepdims=True)
         p = jnp.exp2((s - top) * (SCALE * LOG2E)).astype(jnp.bfloat16)
         if before is not None:
             finish(*before)
-        before = (index, p, pairs[index // GROUP][1])
-        s = later
+        before = (index, p, pair[1])
+        s, pair = later, after
     finish(*before)
     for copy in copies:
         copy.wait()

time: 86.2 us -> 86.2 us (level)
  no operation moved by 1% of the time
where the time goes in v8:
time: 86.2 us; the launch traced here: 86.1 us
  blocking collectives  76.3 us (89%)
  Pallas kernels  9.71 us (11%)
    all_to_all x1, blocking collectives, body(): got = lax.all_to_all(shares, ORDER, 0, 0, tiled=True)  50.6 us
    all_to_all x1, blocking collectives, body(): table = lax.all_to_all(packed, ORDER, 0, 0, tiled=True)  25.7 us
    pallas_call x1, Pallas kernels, body(): pl.pallas_call(attend_kernel, out_shape=jax.ShapeDtypeStruct((BLOCK, HQ *...  7.12 us

profile of v8, /device:TPU:1, one launch (start us, length us, event | category | flops | bytes accessed | tf_op | source)
XLA Modules:
  0.0 86.1 jit_solution(4169942764968527314)
XLA Ops:
  0.0 1.2 %pack.1 = (bf16[2304,128]{1,0:T(8,128)(2,1)S(1)}, bf16[128,1024]{1,0:T(8,128)(2,1)S(1)}, bf16[1024,128]{1,0:T(8,128)(2,1)S(1)}) custom-call(s32[1,8]{1,0:T(1,128)} %sel_hbm.1, s32[8]{0:T(128)} %len_hbm.1, bf16[128,1024]{1,0:T(8,128)(2,1)} %k_hbm.1, bf16[128,1024]{1,0:T(8,128)(2,1)} %v_ref.1), custom_call_target="tpu_custom_call" | custom-call | tf_op jit(solution)/shard_map/pack/pallas_call | solution.py:196
  1.2 25.7 %all_to_all.10 = bf16[128,9,2,128]{3,2,1,0:T(2,128)(2,1)S(1)} all-to-all(bf16[128,9,2,128]{3,2,1,0:T(2,128)(2,1)S(1)} %bitcast.3), channel_id=1, replica_groups=mesh['y_lo'=2,'core'=2,'x'=4,'y_hi'=2,'z'=4] {'z','x','y_lo','y_hi','core'}, dimensions={0} | all-to-all | bytes 1179648 | tf_op jit(solution)/shard_map/all_to_all | solution.py:216
  27.0 1.4 %pick.1 = bf16[128,7,16,128]{3,2,1,0:T(8,128)(2,1)S(1)} custom-call(bf16[2304,128]{1,0:T(8,128)(2,1)S(1)} %bitcast.2), custom_call_target="tpu_custom_call" | custom-call | tf_op jit(solution)/shard_map/pick/pallas_call | solution.py:217
  28.4 0.0 copy-start
  28.4 0.0 copy-start.1
  28.4 50.6 %all_to_all.11.got_ref = bf16[128,7,16,128]{3,2,1,0:T(8,128)(2,1)S(1)} all-to-all(bf16[128,7,16,128]{3,2,1,0:T(8,128)(2,1)S(1)} %pick.1), channel_id=1, replica_groups=mesh['y_lo'=2,'core'=2,'x'=4,'y_hi'=2,'z'=4] {'z','x','y_lo','y_hi','core'}, dimensions={0} | all-to-all | bytes 7340032 | tf_op jit(solution)/shard_map/all_to_all | solution.py:231
  78.9 0.0 copy-done
  78.9 0.0 copy-done.1
  78.9 7.1 %attend.1 = bf16[128,5120]{1,0:T(8,128)(2,1)} custom-call(bf16[128,5120]{1,0:T(8,128)(2,1)S(1)} %copy-done, bf16[1024,128]{1,0:T(8,128)(2,1)S(1)} %get-tuple-element.8.turned_ref, bf16[128,1024]{1,0:T(8,128)(2,1)S(1)} %copy-done.1, bf16[128,1024]{1,0:T(8,128)(2,1)S(1)} %get-tuple-element.9.bias_ref, bf16[128,7,16,128]{3,2,1,0:T(8,128)(2,1)S(1)} %all_to_all.11.got_ref), custom_call_target="tpu_custom_call" | custom-call | tf_op jit(solution)/shard_map/attend/pallas_call | solution.py:232
Async XLA Ops:
  28.4 50.6 %copy-start = (bf16[128,5120]{1,0:T(8,128)(2,1)S(1)}, bf16[128,5120]{1,0:T(8,128)(2,1)}, u32[]{:S(2)}) copy-start(bf16[128,5120]{1,0:T(8,128)(2,1)} %q_ref.1) | copy-start | bytes 3932164
  28.4 50.6 %copy-start.1 = (bf16[128,1024]{1,0:T(8,128)(2,1)S(1)}, bf16[128,1024]{1,0:T(8,128)(2,1)}, u32[]{:S(2)}) copy-start(bf16[128,1024]{1,0:T(8,128)(2,1)} %v_ref.1) | copy-start | bytes 786436
